TPU v7x, 256 devices: a whole 4x4x8 slice. The times are simulated.
256 devices in a mesh: seq: 32 (over y, z), head: 8 (over x, core).
Axes of the slice: x: 4, y: 4, z: 8, core: 2. Of those that a mesh axis runs over, the one named last changes fastest.
Arguments:
- lin_queries: bfloat16 [2, 4096, 8192], P(None, 'seq', 'head'), may hold values from -6 to 6
- lin_keys: bfloat16 [4096, 8192], P('seq', 'head'), may hold values from -6 to 6
- lin_values: bfloat16 [4096, 8192], P('seq', 'head'), may hold values from -20 to 20
- log_decay: float32 [4096, 64], P('seq', 'head'), may hold values from -1 to 0
- norm_gain: float32 [8192], P('head'), may hold values from 0.25 to 1.75
- soft_queries: bfloat16 [2, 4096, 8192], P(None, 'seq', 'head'), may hold values from -6 to 6
- soft_keys: bfloat16 [4096, 1024], P('seq', 'head'), may hold values from -6 to 6
- soft_values: bfloat16 [4096, 1024], P('seq', 'head'), may hold values from -6 to 6
- block_mask: int32 [32, 32], replicated, may hold values from 0 to 1, as said below
Outputs:
- lin_out: bfloat16 [2, 4096, 8192], P(None, 'seq', 'head')
- soft_out: bfloat16 [2, 4096, 8192], P(None, 'seq', 'head')
Inputs may be any that keep to these rules, and one draw needn't show every extreme that they name: block_mask[i, i] is 1 for every block i; entries above the diagonal are not read.
All inputs are finite; a program needn't handle non-finite values.
Results may differ from a plain program's by a relative error of at most 0.02.
Values may be sent and summed in bfloat16 or wider, within the bound.
A program may use at most 128 MiB of HBM per device.

v0:
```python
import math

import jax
import jax.numpy as jnp
from jax import lax
from jax.sharding import PartitionSpec as P

HEAD_COUNT = 64
DH = 128
TILE_SPAN = 128


def carried_in(value, axis, join, neutral):
    count, mine = (lax.axis_size(axis), lax.axis_index(axis))
    pieces = jax.tree.map(lambda part: lax.all_gather(part, axis), value)
    running = jax.tree.map(
        lambda part, zero: jnp.full_like(part, 0) + jnp.asarray(zero, part.dtype), value, neutral
    )

    def hop(position, running):
        longer = join(running, jax.tree.map(lambda part: part[position], pieces))
        return jax.tree.map(lambda new, old: jnp.where(position < mine, new, old), longer, running)

    return lax.fori_loop(0, count - 1, hop, running)


def join_states(earlier, later):
    return (earlier[0] * later[0], later[0][:, None, None] * earlier[1] + later[1])


def local(
    lin_queries,
    lin_keys,
    lin_values,
    log_decay,
    norm_gain,
    soft_queries,
    soft_keys,
    soft_values,
    block_mask,
):
    local_heads = log_decay.shape[1]
    tok_rows = lin_keys.shape[0]
    head_size = lin_keys.shape[1] // local_heads
    queries = lin_queries.reshape(2, tok_rows, local_heads, head_size)
    keys_loc = lin_keys.reshape(tok_rows, local_heads, head_size)
    local_values = lin_values.reshape(tok_rows, local_heads, head_size)
    running = jnp.cumsum(log_decay, axis=0)
    totals = running[-1]
    keys_scaled = (
        keys_loc.astype(jnp.float32) * jnp.exp(totals[None, :] - running)[:, :, None]
    ).astype(jnp.bfloat16)
    update = jnp.einsum(
        "sha,shb->hab", keys_scaled, local_values, preferred_element_type=jnp.float32
    )
    empty_state = jnp.zeros((local_heads, head_size, head_size), jnp.float32)
    own_index = lax.axis_index("seq")
    identity = (jnp.ones((local_heads,), jnp.float32), empty_state)
    prefix_pair = carried_in((jnp.exp(totals), update), "seq", join_states, identity)
    incoming = prefix_pair[1]
    state_b = incoming.astype(jnp.bfloat16)
    from_state = jnp.exp(running)[None, :, :, None] * jnp.einsum(
        "jtha,hab->jthb", queries, state_b, preferred_element_type=jnp.float32
    )
    scores = jnp.einsum("jtha,sha->jhts", queries, keys_loc, preferred_element_type=jnp.float32)
    decay_gap = running.T[:, :, None] - running.T[:, None, :]
    causal = jnp.arange(tok_rows)[:, None] >= jnp.arange(tok_rows)[None, :]
    weights_lin = jnp.where(
        causal[None, None], scores * jnp.exp(jnp.minimum(decay_gap, 0.0))[None], 0.0
    ).astype(jnp.bfloat16)
    in_segment = jnp.einsum(
        "jhts,shb->jthb", weights_lin, local_values, preferred_element_type=jnp.float32
    )
    linear = from_state + in_segment
    squares = jnp.sum(linear * linear, axis=(2, 3))
    square_sum = lax.psum(squares, "head")
    mean_sq = square_sum / (HEAD_COUNT * DH)
    gain_heads = norm_gain.reshape(local_heads, head_size)
    lin_out = (
        linear * lax.rsqrt(mean_sq + 1e-06)[:, :, None, None] * gain_heads[None, None]
    ).astype(jnp.bfloat16)
    lin_out = lin_out.reshape(2, tok_rows, local_heads * head_size)
    soft_in = (soft_queries.astype(jnp.float32) + lin_out.astype(jnp.float32)).astype(jnp.bfloat16)
    kv_heads = soft_keys.shape[1] // head_size
    group_size = local_heads // kv_heads
    soft_q = soft_in.reshape(2, tok_rows, kv_heads, group_size, head_size)
    positions = own_index * tok_rows + jnp.arange(tok_rows)
    block_count = block_mask.shape[0]
    block_ids = jnp.arange(block_count)
    query_blocks = (positions[:, None] // TILE_SPAN == block_ids[None, :]).astype(jnp.float32)
    query_allow = jnp.dot(
        query_blocks,
        block_mask.astype(jnp.float32),
        precision=lax.Precision.HIGHEST,
        preferred_element_type=jnp.float32,
    )
    score_scale = 1.0 / math.sqrt(head_size)
    stat_shape = (2, tok_rows, kv_heads, group_size)
    start_carry = (
        jnp.full(stat_shape, -1e30, jnp.float32),
        jnp.zeros(stat_shape, jnp.float32),
        jnp.zeros(stat_shape + (head_size,), jnp.float32),
    )
    key_piece = lax.all_gather(soft_keys, "seq", axis=0, tiled=True)
    value_piece = lax.all_gather(soft_values, "seq", axis=0, tiled=True)
    key_rows = key_piece.shape[0]
    key_pos = jnp.arange(key_rows)
    key_blocks = (key_pos[:, None] // TILE_SPAN == block_ids[None, :]).astype(jnp.float32)
    block_ok = (
        jnp.dot(
            query_allow,
            key_blocks.T,
            precision=lax.Precision.HIGHEST,
            preferred_element_type=jnp.float32,
        )
        > 0.5
    )
    allowed = block_ok & (key_pos[None, :] <= positions[:, None])

    def update_carry(carry_in):
        run_max, run_sum, accum = carry_in
        key_heads = key_piece.reshape(key_rows, kv_heads, head_size)
        value_heads = value_piece.reshape(key_rows, kv_heads, head_size)
        score_block = (
            jnp.einsum("jtgia,sga->jtgis", soft_q, key_heads, preferred_element_type=jnp.float32)
            * score_scale
        )
        mask_full = allowed[None, :, None, None, :]
        new_max = jnp.maximum(run_max, jnp.max(jnp.where(mask_full, score_block, -1e30), axis=-1))
        probs = jnp.where(mask_full, jnp.exp(score_block - new_max[..., None]), 0.0)
        new_sum = jnp.sum(probs, axis=-1)
        added = jnp.einsum(
            "jtgis,sga->jtgia",
            probs.astype(jnp.bfloat16),
            value_heads,
            preferred_element_type=jnp.float32,
        )
        return (new_max, new_sum, added)

    def keep_carry(carry_in):
        return carry_in

    run_max, run_sum, accum = lax.cond(jnp.any(allowed), update_carry, keep_carry, start_carry)
    soft_out = (
        (accum / run_sum[..., None])
        .astype(jnp.bfloat16)
        .reshape(2, tok_rows, local_heads * head_size)
    )
    return (lin_out, soft_out)


def solution(mesh):
    return jax.shard_map(
        local,
        mesh=mesh,
        in_specs=(
            P(None, "seq", "head"),
            P("seq", "head"),
            P("seq", "head"),
            P("seq", "head"),
            P("head"),
            P(None, "seq", "head"),
            P("seq", "head"),
            P("seq", "head"),
            P(),
        ),
        out_specs=(P(None, "seq", "head"), P(None, "seq", "head")),
        check_vma=False,
    )
```

profile of v0, /device:TPU:56, one launch (start us, length us, event | category | flops | bytes accessed | tf_op | source)
XLA Modules:
  0.0 358.6 jit_solution(7521354241630398443)
XLA Ops:
  9.6 2.0 fusion.33
  13.2 39.1 %all-gather.1 = f32[32,1,8]{2,1,0:T(1,128)S(1)} all-gather(f32[1,1,8]{2,1,0:T(1,128)S(1)} %get-tuple-element.169), channel_id=1, replica_groups=mesh['seq'=32,'head'=8] {'seq'}, dimensions={0}, use_global_device_ids=true | all-gather | bytes 1056 | tf_op jit(solution)/shard_map/all_gather | solution.py:15
  52.3 1.7 copy.105
  55.0 3.0 fusion.54
  59.6 1.3 copy.82
  60.9 90.1 %all-gather.10.cloned.1.call-done = f32[256,128,128]{2,1,0:T(8,128)} async-done(((f32[8,128,128]{2,1,0:T(8,128)}), f32[256,128,128]{2,1,0:T(8,128)}) %all-gather.10.cloned.1.call-update) | async-done | bytes 16777232 | tf_op jit(solution)/shard_map/all_gather | solution.py:15
  151.0 37.8 %while.14 = (s32[]{:T(128)}, f32[8,128,128]{2,1,0:T(8,128)S(1)}, s32[]{:T(128)}, f32[32,8]{1,0:T(8,128)S(1)}, f32[32,8,128,128]{3,2,1,0:T(8,128)}, /*index=5*/s32[]{:T(128)}, s32[]{:T(128)}) while((s32[]{:T(128)}, f32[8,128,128]{2,1,0:T(8,128)S(1)}, s32[]{:T(128)}, f32[32,8]{1,0:T(8,128)S(1)}, f32[32,8,128,128]{3,2,1,0:T(8,128)}, ...), condition=%wide.region_2.3_spmd.clone, body=%wide.region_1.2_spmd.clone.sunk | while | flops 524292 | bytes 1573073 | solution.py:24
  153.4 1.2 fusion.61
  154.6 1.2 fusion.61
  155.8 1.2 fusion.61
  157.1 1.2 fusion.61
  158.3 1.2 fusion.61
  159.5 1.2 fusion.61
  160.7 1.2 fusion.61
  165.6 1.2 fusion.61
  166.8 1.2 fusion.61
  169.2 1.2 fusion.61
  170.5 1.2 fusion.61
  174.1 1.2 fusion.61
  181.4 1.2 fusion.61
  185.1 1.2 fusion.61
  186.3 1.2 fusion.61
  187.5 1.2 fusion.61
  189.1 1.6 multiply_reduce_fusion
  190.7 14.2 %psum.7 = f32[2,128]{1,0:T(2,128)S(1)} all-reduce(f32[2,128]{1,0:T(2,128)S(1)} %get-tuple-element.170), channel_id=1, replica_groups=mesh['seq'=32,'head'=8] {'head'}, use_global_device_ids=true, to_apply=%region_4.5 | all-reduce | flops 256 | bytes 2048 | tf_op jit(solution)/shard_map/psum | solution.py:76
  207.0 21.9 %all-gather.6.cloned.1.call-done = bf16[4096,128]{1,0:T(8,128)(2,1)} async-done(((bf16[128,128]{1,0:T(8,128)(2,1)}), bf16[4096,128]{1,0:T(8,128)(2,1)}) %all-gather.6.cloned.1.call-update) | async-done | bytes 1048592 | tf_op jit(solution)/shard_map/all_gather | solution.py:104
  228.9 76.4 %all-gather.8.cloned.1.call-done = bf16[4096,128]{1,0:T(8,128)(2,1)} async-done(((bf16[128,128]{1,0:T(8,128)(2,1)}), bf16[4096,128]{1,0:T(8,128)(2,1)}) %all-gather.8.cloned.1.call-update) | async-done | bytes 1048592 | tf_op jit(solution)/shard_map/all_gather | solution.py:105
  305.4 44.9 %conditional.1 = (f32[2,128,1,8]{1,3,0,2:T(8,128)S(1)}, f32[2,128,1,8,128]{4,1,3,0,2:T(8,128)S(1)}) conditional(s32[]{:T(128)} %convert_element_type.44, () %tuple.31, (pred[128,4096]{1,0:T(8,128)(4,1)}, bf16[2,128,1024]{1,2,0:T(8,128)(2,1)S(1)}, bf16[4096,128]{1,0:T(8,128)(2,1)}, bf16[4096,128]{1,0:T(8,128)(2,1)}) %tuple.32), branch_computations={%region_6.7_spmd, %region_7.10_spmd} | conditional | flops 4387239936 | bytes 111198248 | solution.py:143
  305.4 1.9 copy.83
  307.3 14.5 %fusion = (f32[2,128,8]{1,2,0:T(8,128)S(1)}, f32[4096,2,128,8]{2,0,3,1:T(8,128)}) fusion(pred[128,4096]{0,1:T(8,128)(4,1)S(1)} %copy.83, bf16[2,128,8,128]{1,3,2,0:T(8,128)(2,1)S(1)} %bitcast.134, bf16[4096,128]{1,0:T(8,128)(2,1)} %get-tuple-element.103), kind=kOutput, calls=%fused_computation.2 | convolution fusion | flops 2172647424 | bytes 35659776 | tf_op jit(solution)/shard_map/cond/branch_1_fun/jtgia,sga->jtgis/dot_general | solution.py:125
  321.8 14.4 %fusion.9 = f32[2,128,1,8,128]{4,1,3,0,2:T(8,128)S(1)} fusion(f32[4096,2,128,8]{2,0,3,1:T(8,128)} %get-tuple-element.165, f32[2,128,8]{1,2,0:T(8,128)S(1)} %broadcast_maximum_fusion, pred[128,4096]{0,1:T(8,128)(4,1)S(1)} %copy.83, bf16[4096,128]{1,0:T(8,128)(2,1)S(1)} %copy-done.1), kind=kOutput, calls=%fused_computation.10 | convolution fusion | flops 2181038080 | bytes 36184064 | tf_op jit(solution)/shard_map/cond/branch_1_fun/jtgis,sga->jtgia/dot_general | solution.py:132
  336.2 14.1 %fusion.4 = f32[2,128,8]{1,2,0:T(8,128)S(1)} fusion(f32[4096,2,128,8]{2,0,3,1:T(8,128)} %get-tuple-element.165, f32[2,128,8]{1,2,0:T(8,128)S(1)} %broadcast_maximum_fusion, pred[128,4096]{0,1:T(8,128)(4,1)S(1)} %copy.83), kind=kLoop, calls=%fused_computation.6 | loop fusion | flops 33552384 | bytes 34095104 | tf_op jit(solution)/shard_map/cond/branch_1_fun/reduce_sum | solution.py:131
  (81 shorter events, 28.0 us)
Async XLA Ops:
  7.2 181.6 %copy-start = (bf16[2,128,1024]{2,1,0:T(8,128)(2,1)S(1)}, bf16[2,128,1024]{2,1,0:T(8,128)(2,1)}, u32[]{:S(2)}) copy-start(bf16[2,128,1024]{2,1,0:T(8,128)(2,1)} %param.13) | copy-start | bytes 1572868
  7.2 143.8 %all-gather.10.cloned.1.call-start = ((), (), s32[]{:S(2)}) async-start(), calls=%async_computation.2 | async-start | bytes 17301504 | tf_op jit(solution)/shard_map/all_gather | solution.py:15
  11.6 217.4 %all-gather.6.cloned.1.call-start = ((), (), s32[]{:S(2)}) async-start(), calls=%async_computation | async-start | bytes 1081344 | tf_op jit(solution)/shard_map/all_gather | solution.py:104
  12.3 293.1 %all-gather.8.cloned.1.call-start = ((), (), s32[]{:S(2)}) async-start(), calls=%async_computation.1 | async-start | bytes 1081344 | tf_op jit(solution)/shard_map/all_gather | solution.py:105
  307.2 14.5 %copy-start.1 = (bf16[4096,128]{1,0:T(8,128)(2,1)S(1)}, bf16[4096,128]{1,0:T(8,128)(2,1)}, u32[]{:S(2)}) copy-start(bf16[4096,128]{1,0:T(8,128)(2,1)} %get-tuple-element.105) | copy-start | bytes 3145732 | tf_op jit(solution)/shard_map/cond
Sparse Core Ops, SparseCore 0:
  11.7 139.2 all-gather.9
  153.5 75.3 all-gather.5
  231.5 73.7 all-gather.7
where the time goes:
time: 363 us; the launch traced here: 359 us
  waiting for transfers between devices  190 us (52%)
  other arithmetic  53.3 us (15%)
  blocking collectives  53.3 us (15%)
  matrix products  36.7 us (10%)
  between operations  14.5 us (4%)
  local copies, waits for them, and re-layouts  9.83 us (3%)
    all_gather x1, waiting for transfers between devices, carried_in(): pieces = jax.tree.map(lambda part: lax.all_gather(part, axis), value)  90.1 us
    all_gather x1, waiting for transfers between devices, local(): value_piece = lax.all_gather(soft_values, 'seq', axis=0, tiled=True)  76.4 us
    all_gather x1, blocking collectives, carried_in(): pieces = jax.tree.map(lambda part: lax.all_gather(part, axis), value)  39.1 us
    select_n x31, other arithmetic, hop(): jnp.where(position < mine, new, old)  36.5 us
    all_gather x1, waiting for transfers between devices, local(): key_piece = lax.all_gather(soft_keys, 'seq', axis=0, tiled=True)  21.9 us
    dot_general x1, matrix products, update_carry(): jnp.einsum('jtgia,sga->jtgis', soft_q, key_heads, preferred_element_type=...  14.5 us
    dot_general x1, matrix products, update_carry(): jnp.einsum('jtgis,sga->jtgia', probs.astype(jnp.bfloat16), value_heads, p...  14.4 us
    psum x1, blocking collectives, local(): square_sum = lax.psum(squares, 'head')  14.2 us
  transfers between devices with their start and end apart: 3, of which 3 were waited for; matrix products, arithmetic and copies ran while one was open for 14% of the time, Pallas kernels for 0%

commit v1 on v0

v1 whole, which is shorter than its diff:
```python
import math

import jax
import jax.numpy as jnp
from jax import lax
from jax.experimental import pallas as pl
from jax.experimental.pallas import tpu as pltpu
from jax.sharding import PartitionSpec as P

MESH = pl.DeviceIdType.MESH
HI = lax.Precision.HIGHEST
F32 = jnp.float32
BF16 = jnp.bfloat16

FEATURES = 8192
DH = 128
TOK = 128
HEADS = 8
NY, NZ, NX = 4, 8, 8
NSEQ = NY * NZ
NEG = -1e30
STEP_BLOCKS = 4
STEP = STEP_BLOCKS * TOK
SCALE = math.log2(math.e) / math.sqrt(DH)


def dot_t(a, b, **kw):
    return lax.dot_general(a, b, (((1,), (1,)), ((), ())), preferred_element_type=F32, **kw)


def dot_0(a, b, **kw):
    return lax.dot_general(a, b, (((0,), (0,)), ((), ())), preferred_element_type=F32, **kw)


def dot(a, b, **kw):
    return jnp.dot(a, b, preferred_element_type=F32, **kw)


def cols(h):
    return pl.ds(pl.multiple_of(h * DH, DH), DH)


def linear_kernel(
    lq_hbm, lk_hbm, lv_hbm, ld_hbm, gain_ref, sk, sv,
    lin_out, kv,
    lq, lk, lv, ld, ks, u_send, u_recv, dec_send, dec_recv, drow_send, drow_recv,
    t_send, t_recv, p_send, st, lin, sq_send, sq_recv,
    in_sem, own_sem, kv_send, kv_recv, u_ss, u_rs, d_ss, d_rs, w_ss, w_rs,
    t_ss, t_rs, p_ss, p_rs, q_ss, q_rs,
):
    me = lax.axis_index("seq")
    hd = lax.axis_index("head")
    y, z = me // NZ, me % NZ

    def zpeer(i):
        return y * NZ + (z + i + NZ) % NZ

    def ypeer(i):
        return ((y + i + NY) % NY) * NZ + z

    def to_seq(src, dst, ssem, rsem, dev):
        return pltpu.make_async_remote_copy(
            src_ref=src, dst_ref=dst, send_sem=ssem, recv_sem=rsem,
            device_id={"seq": dev}, device_id_type=MESH,
        )

    loads = [
        pltpu.make_async_copy(a, b, in_sem.at[i])
        for i, (a, b) in enumerate(((ld_hbm, ld), (lk_hbm, lk), (lv_hbm, lv), (lq_hbm, lq)))
    ]
    for c in loads:
        c.start()

    barrier = pltpu.get_barrier_semaphore()
    for i in range(1, NZ):
        pl.semaphore_signal(barrier, inc=1, device_id={"seq": zpeer(i)}, device_id_type=MESH)
    for i in range(1, NY):
        pl.semaphore_signal(barrier, inc=1, device_id={"seq": ypeer(i)}, device_id_type=MESH)
    for i in range(1, NX):
        pl.semaphore_signal(barrier, inc=1, device_id={"head": (hd + i) % NX}, device_id_type=MESH)

    loads[0].wait()
    row = lax.broadcasted_iota(jnp.int32, (TOK, TOK), 0)
    col = lax.broadcasted_iota(jnp.int32, (TOK, TOK), 1)
    tril = (row >= col).astype(F32)
    spread = (
        lax.broadcasted_iota(jnp.int32, (HEADS, DH), 0) == lax.broadcasted_iota(jnp.int32, (HEADS, DH), 1)
    ).astype(F32)
    cum = dot(tril, dot(ld[...], spread, precision=HI), precision=HI)
    cum_t = cum.T
    total = cum[TOK - 1 : TOK, :]
    dec_send[...] = jnp.broadcast_to(total, (8, DH))
    dec_recv[pl.ds(z, 1)] = jnp.broadcast_to(total, (1, 8, DH))

    pl.semaphore_wait(barrier, NZ + NY + NX - 3)

    sends = []

    def start(c):
        c.start()
        sends.append(c)

    for i in range(1, NZ):
        start(to_seq(dec_send, dec_recv.at[z], d_ss.at[i], d_rs.at[z], zpeer(i)))

    own = [pltpu.make_async_copy(a, kv.at[me, k], own_sem.at[k]) for k, a in enumerate((sk, sv))]
    for c in own:
        c.start()
    kv_count = [0]
    reach_right = (4, 3)
    reach_left = (3, 4)

    def kv_start(src, b, k, dev):
        n = kv_count[0]
        kv_count[0] += 1
        start(to_seq(src, kv.at[b, k], kv_send.at[n], kv_recv.at[b, k], dev))

    def kv_wait(b, k):
        to_seq(kv.at[b, k], kv.at[b, k], kv_send.at[0], kv_recv.at[b, k], me).wait_recv()

    def kv_own():
        for k, a in enumerate((sk, sv)):
            kv_start(a, me, k, zpeer(1))
            kv_start(a, me, k, zpeer(-1))
            kv_start(a, me, k, ypeer(1))
            kv_start(a, me, k, ypeer(-1))

    def kv_step(s):
        for k in range(2):
            if s <= reach_right[k]:
                b = zpeer(-s)
                kv_wait(b, k)
                if s < reach_right[k]:
                    kv_start(kv.at[b, k], b, k, zpeer(1))
                kv_start(kv.at[b, k], b, k, ypeer(1))
                kv_start(kv.at[b, k], b, k, ypeer(-1))
            if s <= reach_left[k]:
                b = zpeer(s)
                kv_wait(b, k)
                if s < reach_left[k]:
                    kv_start(kv.at[b, k], b, k, zpeer(-1))
                kv_start(kv.at[b, k], b, k, ypeer(1))
                kv_start(kv.at[b, k], b, k, ypeer(-1))

    def block(dy, dz):
        return ((y + dy + NY) % NY) * NZ + (z + dz + NZ) % NZ

    def kv_forward(dz):
        kv_wait(block(-1, dz), 0)
        kv_start(kv.at[block(-1, dz), 0], block(-1, dz), 0, ypeer(1))
        kv_wait(block(1, dz), 1)
        kv_start(kv.at[block(1, dz), 1], block(1, dz), 1, ypeer(-1))

    kv_own()

    loads[1].wait()
    fade = jnp.exp(total - cum)
    for h in range(HEADS):
        hs = slice(h * DH, (h + 1) * DH)
        ks[:, hs] = (lk[:, hs].astype(F32) * fade[:, h : h + 1]).astype(BF16)
    loads[2].wait()
    for i in (4, 3, 5, 2, 6, 1, 7, 0):
        h = (z + i) % NZ
        u = dot_0(ks[:, cols(h)], lv[:, cols(h)]).astype(BF16)
        if i:
            u_send[pl.ds(h, 1)] = u[None]
            start(to_seq(u_send.at[h], u_recv.at[z], u_ss.at[i], u_rs.at[z], zpeer(i)))
        else:
            u_recv[pl.ds(h, 1)] = u[None]

    kv_step(1)

    for i in range(1, NZ):
        src = (z - i + NZ) % NZ
        to_seq(dec_send, dec_recv.at[src], d_ss.at[i], d_rs.at[src], zpeer(i)).wait_recv()
    row_sum = jnp.sum(dec_recv[...], axis=0)
    drow_send[...] = row_sum
    drow_recv[pl.ds(y, 1)] = row_sum[None]
    for i in range(1, NY):
        start(to_seq(drow_send, drow_recv.at[y], w_ss.at[i], w_rs.at[y], ypeer(i)))

    loads[3].wait()
    causal = row >= col
    for h in range(HEADS):
        hs = slice(h * DH, (h + 1) * DH)
        q = lq[:, :, hs].reshape(2 * TOK, DH)
        score = dot_t(q, lk[:, hs])
        gap = jnp.exp(jnp.minimum(cum[:, h : h + 1] - cum_t[h : h + 1, :], 0.0))
        gap = jnp.where(causal, gap, 0.0)
        w = (score.reshape(2, TOK, TOK) * gap[None]).astype(BF16).reshape(2 * TOK, TOK)
        lin[h] = dot(w, lv[:, hs])
        if h == 3:
            kv_step(2)

    lane = lax.broadcasted_iota(jnp.int32, (8, DH), 1)

    def of_head(v):
        return jnp.exp(jnp.sum(jnp.where(lane == z, v, 0.0), axis=1, keepdims=True)[:1])

    decay = [of_head(dec_recv[i]) for i in range(NZ)]
    for i in range(1, NZ):
        src = (z - i + NZ) % NZ
        to_seq(u_send.at[0], u_recv.at[src], u_ss.at[i], u_rs.at[src], zpeer(i)).wait_recv()
    t = u_recv[0].astype(F32)
    for i in range(1, NZ):
        t = t * decay[i] + u_recv[i].astype(F32)
    t_send[...] = t.astype(BF16)
    t_recv[pl.ds(y, 1)] = t.astype(BF16)[None]
    for i in (2, 1, 3):
        start(to_seq(t_send, t_recv.at[y], t_ss.at[i], t_rs.at[y], ypeer(i)))

    kv_step(3)
    kv_forward(0)

    for i in range(1, NY):
        src = (y - i + NY) % NY
        to_seq(drow_send, drow_recv.at[src], w_ss.at[i], w_rs.at[src], ypeer(i)).wait_recv()
        to_seq(t_send, t_recv.at[src], t_ss.at[i], t_rs.at[src], ypeer(i)).wait_recv()
    s = jnp.zeros((DH, DH), F32)
    for i in range(NY - 1):
        s = jnp.where(i < y, s * of_head(drow_recv[i]) + t_recv[i].astype(F32), s)
    for i in range(NZ):
        p_send[i] = s.astype(BF16)
        if i < NZ - 1:
            s = s * decay[i] + u_recv[i].astype(F32)
    for i in (4, 3, 5, 2, 6, 1, 7):
        d = (z + i) % NZ
        start(to_seq(p_send.at[d], st.at[z], p_ss.at[i], p_rs.at[z], zpeer(i)))
    st[pl.ds(z, 1)] = p_send[pl.ds(z, 1)]

    kv_step(4)
    for dz in (1, -1, 2, -2):
        kv_forward(dz)

    for i in range(1, NZ):
        src = (z - i + NZ) % NZ
        to_seq(p_send.at[0], st.at[src], p_ss.at[i], p_rs.at[src], zpeer(i)).wait_recv()

    ecum = jnp.exp(cum)
    squares = jnp.zeros((2 * TOK, DH), F32)
    for h in range(HEADS):
        hs = slice(h * DH, (h + 1) * DH)
        q = lq[:, :, hs].reshape(2 * TOK, DH)
        f = dot(q, st[h]).reshape(2, TOK, DH) * ecum[:, h : h + 1][None]
        full = lin[h] + f.reshape(2 * TOK, DH)
        lin[h] = full
        squares = squares + full * full
    sq = dot_t(jnp.ones((8, DH), F32), squares, precision=HI)
    sq_send[...] = sq
    sq_recv[pl.ds(hd, 1)] = sq[None]
    for i in range(1, NX):
        start(
            pltpu.make_async_remote_copy(
                src_ref=sq_send, dst_ref=sq_recv.at[hd], send_sem=q_ss.at[i], recv_sem=q_rs.at[hd],
                device_id={"head": (hd + i) % NX}, device_id_type=MESH,
            )
        )
    for dz in (3, -3, 4):
        kv_forward(dz)
    for i in range(1, NX):
        src = (hd - i + NX) % NX
        pltpu.make_async_remote_copy(
            src_ref=sq_send, dst_ref=sq_recv.at[src], send_sem=q_ss.at[i], recv_sem=q_rs.at[src],
            device_id={"head": src}, device_id_type=MESH,
        ).wait_recv()
    mean = jnp.sum(sq_recv[...], axis=0) * (1.0 / FEATURES)
    inv = dot_0(lax.rsqrt(mean + 1e-6), jnp.full((8, DH), 0.125, F32), precision=HI)
    for h in range(HEADS):
        hs = slice(h * DH, (h + 1) * DH)
        res = lin[h] * inv * gain_ref[hs][None, :]
        lin_out[:, :, hs] = res.astype(BF16).reshape(2, TOK, DH)

    for dz in range(NZ):
        kv_wait(block(-1, dz), 1)
        kv_wait(block(1, dz), 0)
        kv_wait(block(2, dz), 0)
        kv_wait(block(2, dz), 1)
    for c in own:
        c.wait()
    for c in sends:
        c.wait_send()


def linear_part(lq, lk, lv, ld, gain, sk, sv):
    hbm = pl.BlockSpec(memory_space=pl.ANY)
    vmem = pl.BlockSpec(memory_space=pltpu.VMEM)
    dma = pltpu.SemaphoreType.DMA
    V = pltpu.VMEM
    mat = (DH, DH)
    return pl.pallas_call(
        linear_kernel,
        out_shape=(
            jax.ShapeDtypeStruct((2, TOK, HEADS * DH), BF16),
            jax.ShapeDtypeStruct((NSEQ, 2, TOK, DH), BF16),
        ),
        in_specs=[hbm, hbm, hbm, hbm, vmem, hbm, hbm],
        out_specs=(vmem, hbm),
        scratch_shapes=[
            V((2, TOK, HEADS * DH), BF16),
            V((TOK, HEADS * DH), BF16),
            V((TOK, HEADS * DH), BF16),
            V((TOK, HEADS), F32),
            V((TOK, HEADS * DH), BF16),
            V((NZ,) + mat, BF16),
            V((NZ,) + mat, BF16),
            V((8, DH), F32),
            V((NZ, 8, DH), F32),
            V((8, DH), F32),
            V((NY, 8, DH), F32),
            V(mat, BF16),
            V((NY,) + mat, BF16),
            V((NZ,) + mat, BF16),
            V((HEADS,) + mat, BF16),
            V((HEADS, 2 * TOK, DH), F32),
            V((8, 2 * TOK), F32),
            V((NX, 8, 2 * TOK), F32),
            dma((4,)),
            dma((2,)),
            dma((62,)),
            dma((NSEQ, 2)),
            dma((NZ,)), dma((NZ,)),
            dma((NZ,)), dma((NZ,)),
            dma((NY,)), dma((NY,)),
            dma((NY,)), dma((NY,)),
            dma((NZ,)), dma((NZ,)),
            dma((NX,)), dma((NX,)),
        ],
        compiler_params=pltpu.CompilerParams(
            collective_id=0, has_side_effects=True, vmem_limit_bytes=32 * 2**20
        ),
        cost_estimate=pl.CostEstimate(flops=240_000_000, bytes_accessed=5_000_000, transcendentals=300_000),
        name="linear_and_gather",
    )(lq, lk, lv, ld, gain, sk, sv)


def softmax_kernel(
    mask, lin_ref, sq_ref, kv,
    lin_out, soft_out,
    order, kaug, vaug, qaug, m_ref, acc, k_sem, v_sem,
):
    me = lax.axis_index("seq")
    order[0] = me

    def scan(b, n):
        ok = jnp.logical_and(mask[me, b] == 1, b < me)

        @pl.when(ok)
        def _():
            order[n] = b

        return n + ok.astype(jnp.int32)

    count = lax.fori_loop(0, NSEQ, scan, jnp.int32(1))
    steps = (count + STEP_BLOCKS - 1) // STEP_BLOCKS

    def pad(i, c):
        order[i] = me
        return c

    lax.fori_loop(count, steps * STEP_BLOCKS, pad, 0)

    def rows(i, size=TOK):
        return pl.ds(pl.multiple_of(i * size, size), size)

    def copies(i):
        b = order[i]
        return (
            pltpu.make_async_copy(kv.at[b, 0], kaug.at[rows(i), pl.ds(0, DH)], k_sem.at[i]),
            pltpu.make_async_copy(kv.at[b, 1], vaug.at[rows(i), pl.ds(0, DH)], v_sem.at[i]),
        )

    def load(i, c):
        for x in copies(i):
            x.start()
        return c

    lax.fori_loop(0, steps * STEP_BLOCKS, load, 0)

    row = lax.broadcasted_iota(jnp.int32, (TOK, TOK), 0)
    col = lax.broadcasted_iota(jnp.int32, (TOK, TOK), 1)

    def bias(i, c):
        kaug[rows(i), DH:] = jnp.where(i < count, 0.0, jnp.full((TOK, TOK), NEG, F32)).astype(BF16)
        vaug[rows(i), DH:] = jnp.ones((TOK, DH), BF16)
        return c

    lax.fori_loop(0, steps * STEP_BLOCKS, bias, 0)
    kaug[:TOK, DH:] = jnp.where(row <= col, 0.0, NEG).astype(BF16)
    pick = (row == col).astype(BF16)
    for h in range(HEADS):
        hs = slice(h * DH, (h + 1) * DH)
        for j in range(2):
            lin = lin_ref[j, :, hs]
            q = (sq_ref[j, :, hs].astype(F32) + lin.astype(F32)) * SCALE
            qaug[h, j * TOK : (j + 1) * TOK, :DH] = q.astype(BF16)
            qaug[h, j * TOK : (j + 1) * TOK, DH:] = pick
            lin_out[j, :, hs] = lin

    def step(i, first):
        for n in range(STEP_BLOCKS):
            for x in copies(i * STEP_BLOCKS + n):
                x.wait()
        for h in range(HEADS):
            s = dot_t(qaug[h], kaug[rows(i, STEP), :])
            top = jnp.max(s, axis=1, keepdims=True)
            if not first:
                top = jnp.maximum(m_ref[h][:, :1], top)
                keep = jnp.exp2(m_ref[h] - top)
            p = jnp.exp2(s - top).astype(BF16)
            new = dot(p, vaug[rows(i, STEP), :])
            if first:
                acc[h] = new
            else:
                acc[h, :, :DH] = acc[h, :, :DH] * keep + new[:, :DH]
                acc[h, :, DH:] = acc[h, :, DH:] * keep + new[:, DH:]
            m_ref[h] = jnp.broadcast_to(top, (2 * TOK, DH))

    step(0, True)

    def rest(i, c):
        step(i, False)
        return c

    lax.fori_loop(1, steps, rest, 0)
    for h in range(HEADS):
        hs = slice(h * DH, (h + 1) * DH)
        out = (acc[h, :, :DH] / acc[h, :, DH:]).astype(BF16)
        soft_out[:, :, hs] = out.reshape(2, TOK, DH)


def softmax_part(mask, lin, sq, kv):
    hbm = pl.BlockSpec(memory_space=pl.ANY)
    vmem = pl.BlockSpec(memory_space=pltpu.VMEM)
    V = pltpu.VMEM
    out = jax.ShapeDtypeStruct((2, TOK, HEADS * DH), BF16)
    return pl.pallas_call(
        softmax_kernel,
        out_shape=(out, out),
        in_specs=[pl.BlockSpec(memory_space=pltpu.SMEM), vmem, vmem, hbm],
        out_specs=(vmem, vmem),
        scratch_shapes=[
            pltpu.SMEM((NSEQ,), jnp.int32),
            V((NSEQ * TOK, 2 * DH), BF16),
            V((NSEQ * TOK, 2 * DH), BF16),
            V((HEADS, 2 * TOK, 2 * DH), BF16),
            V((HEADS, 2 * TOK, DH), F32),
            V((HEADS, 2 * TOK, 2 * DH), F32),
            pltpu.SemaphoreType.DMA((NSEQ,)),
            pltpu.SemaphoreType.DMA((NSEQ,)),
        ],
        compiler_params=pltpu.CompilerParams(vmem_limit_bytes=40 * 2**20),
        cost_estimate=pl.CostEstimate(flops=6_000_000_000, bytes_accessed=5_000_000, transcendentals=6_000_000),
        name="softmax_attention",
    )(mask, lin, sq, kv)


def local(lin_queries, lin_keys, lin_values, log_decay, norm_gain, soft_queries, soft_keys, soft_values, block_mask):
    lin, kv = linear_part(lin_queries, lin_keys, lin_values, log_decay, norm_gain, soft_keys, soft_values)
    return softmax_part(block_mask, lin, soft_queries, kv)


def solution(mesh):
    return jax.shard_map(
        local,
        mesh=mesh,
        in_specs=(
            P(None, "seq", "head"),
            P("seq", "head"),
            P("seq", "head"),
            P("seq", "head"),
            P("head"),
            P(None, "seq", "head"),
            P("seq", "head"),
            P("seq", "head"),
            P(),
        ),
        out_specs=(P(None, "seq", "head"), P(None, "seq", "head")),
        check_vma=False,
    )
```

time: 363 us -> 60.3 us (0.17)
  the two profiles are of different devices: /device:TPU:56 before, /device:TPU:249 now
where the time goes in v1:
time: 60.3 us; the launch traced here: 59.8 us
  Pallas kernels  51.5 us (85%)
  local copies, waits for them, and re-layouts  7.68 us (13%)
  between operations  0.66 us (1%)
    pallas_call x1, Pallas kernels, linear_part(): pl.pallas_call(linear_kernel, out_shape=(jax.ShapeDtypeStruct((2, TOK, HE...  34.4 us
    pallas_call x1, Pallas kernels, softmax_part(): pl.pallas_call(softmax_kernel, out_shape=(out, out), in_specs=[pl.BlockSp...  17 us
    unnamed x17, local copies, waits for them, and re-layouts  7.68 us

profile of v1, /device:TPU:249, one launch (start us, length us, event | category | flops | bytes accessed | tf_op | source)
XLA Modules:
  0.0 59.8 jit_solution(13795381670800655392)
XLA Ops:
  0.6 0.8 %copy.11.ld_hbm = f32[128,8]{1,0:T(8,128)S(1)} copy(f32[128,8]{0,1:T(8,128)} %param.12) | data formatting | bytes 8192 | tf_op args[3]
  1.4 0.0 copy-start
  1.4 1.0 %copy-done = bf16[2,128,1024]{2,1,0:T(8,128)(2,1)S(1)} copy-done((bf16[2,128,1024]{2,1,0:T(8,128)(2,1)S(1)}, bf16[2,128,1024]{2,1,0:T(8,128)(2,1)}, u32[]{:S(2)}) %copy-start) | copy-done | bytes 524312
  2.5 0.0 copy-start.1
  2.5 0.9 %copy-done.1 = bf16[128,1024]{1,0:T(8,128)(2,1)S(1)} copy-done((bf16[128,1024]{1,0:T(8,128)(2,1)S(1)}, bf16[128,1024]{1,0:T(8,128)(2,1)}, u32[]{:S(2)}) %copy-start.1) | copy-done | bytes 262168
  3.4 0.0 copy-start.2
  3.4 0.9 %copy-done.2 = bf16[128,1024]{1,0:T(8,128)(2,1)S(1)} copy-done((bf16[128,1024]{1,0:T(8,128)(2,1)S(1)}, bf16[128,1024]{1,0:T(8,128)(2,1)}, u32[]{:S(2)}) %copy-start.2) | copy-done | bytes 262168
  4.4 0.0 copy-start.3
  4.4 0.8 %copy-done.3 = bf16[128,128]{1,0:T(8,128)(2,1)S(1)} copy-done((bf16[128,128]{1,0:T(8,128)(2,1)S(1)}, bf16[128,128]{1,0:T(8,128)(2,1)}, u32[]{:S(2)}) %copy-start.3) | copy-done | bytes 32792
  5.1 0.0 copy-start.4
  5.1 0.8 %copy-done.4 = bf16[128,128]{1,0:T(8,128)(2,1)S(1)} copy-done((bf16[128,128]{1,0:T(8,128)(2,1)S(1)}, bf16[128,128]{1,0:T(8,128)(2,1)}, u32[]{:S(2)}) %copy-start.4) | copy-done | bytes 32792
  5.9 0.0 copy-start.5
  5.9 0.7 %copy-done.5 = f32[1024]{0:T(1024)S(1)} copy-done((f32[1024]{0:T(1024)S(1)}, f32[1024]{0:T(1024)}, u32[]{:S(2)}) %copy-start.5) | copy-done | bytes 4120
  6.6 34.4 %linear_and_gather.1 = (bf16[2,128,1024]{2,1,0:T(8,128)(2,1)S(1)}, bf16[32,2,128,128]{3,2,1,0:T(8,128)(2,1)S(1)}) custom-call(bf16[2,128,1024]{2,1,0:T(8,128)(2,1)S(1)} %copy-done, bf16[128,1024]{1,0:T(8,128)(2,1)S(1)} %copy-done.1, bf16[128,1024]{1,0:T(8,128)(2,1)S(1)} %copy-done.2, f32[128,8]{1,0:T(8,128)S(1)} %copy.11.ld_hbm, f32[1024]{0:T(1024)S(1)} %copy-done.5, ...), custom_call_target="tpu_custom_call" | custom-call | flops 240000000 | bytes 5000000 | tf_op jit(solution)/shard_map/linear_and_gather/pallas_call | solution.py:290
  41.0 0.0 copy-start.6
  41.0 1.0 %copy-done.6 = bf16[2,128,1024]{2,1,0:T(8,128)(2,1)S(1)} copy-done((bf16[2,128,1024]{2,1,0:T(8,128)(2,1)S(1)}, bf16[2,128,1024]{2,1,0:T(8,128)(2,1)}, u32[]{:S(2)}) %copy-start.6) | copy-done | bytes 524312
  42.0 0.0 copy-start.7
  42.0 0.7 %copy-done.7 = s32[32,32]{1,0:T(8,128)S(1)} copy-done((s32[32,32]{1,0:T(8,128)S(1)}, s32[32,32]{1,0:T(8,128)}, u32[]{:S(2)}) %copy-start.7) | copy-done | bytes 4120
  42.7 17.0 %softmax_attention.1 = (bf16[2,128,1024]{2,1,0:T(8,128)(2,1)}, bf16[2,128,1024]{2,1,0:T(8,128)(2,1)}) custom-call(s32[32,32]{1,0:T(8,128)S(1)} %copy-done.7, bf16[2,128,1024]{2,1,0:T(8,128)(2,1)S(1)} %get-tuple-element.4.lin_ref, bf16[2,128,1024]{2,1,0:T(8,128)(2,1)S(1)} %copy-done.6, bf16[32,2,128,128]{3,2,1,0:T(8,128)(2,1)S(1)} %get-tuple-element.5.kv), custom_call_target="tpu_custom_call" | custom-call | flops 6000000000 | bytes 5000000 | tf_op jit(solution)/shard_map/softmax_attention/pallas_call | solution.py:436
Async XLA Ops:
  1.4 1.0 %copy-start = (bf16[2,128,1024]{2,1,0:T(8,128)(2,1)S(1)}, bf16[2,128,1024]{2,1,0:T(8,128)(2,1)}, u32[]{:S(2)}) copy-start(bf16[2,128,1024]{2,1,0:T(8,128)(2,1)} %lq_hbm.1) | copy-start | bytes 1572868
  2.5 0.9 %copy-start.1 = (bf16[128,1024]{1,0:T(8,128)(2,1)S(1)}, bf16[128,1024]{1,0:T(8,128)(2,1)}, u32[]{:S(2)}) copy-start(bf16[128,1024]{1,0:T(8,128)(2,1)} %lk_hbm.1) | copy-start | bytes 786436
  3.4 0.9 %copy-start.2 = (bf16[128,1024]{1,0:T(8,128)(2,1)S(1)}, bf16[128,1024]{1,0:T(8,128)(2,1)}, u32[]{:S(2)}) copy-start(bf16[128,1024]{1,0:T(8,128)(2,1)} %lv_hbm.1) | copy-start | bytes 786436
  4.4 0.8 %copy-start.3 = (bf16[128,128]{1,0:T(8,128)(2,1)S(1)}, bf16[128,128]{1,0:T(8,128)(2,1)}, u32[]{:S(2)}) copy-start(bf16[128,128]{1,0:T(8,128)(2,1)} %sk.1) | copy-start | bytes 98308
  5.1 0.8 %copy-start.4 = (bf16[128,128]{1,0:T(8,128)(2,1)S(1)}, bf16[128,128]{1,0:T(8,128)(2,1)}, u32[]{:S(2)}) copy-start(bf16[128,128]{1,0:T(8,128)(2,1)} %sv.1) | copy-start | bytes 98308
  5.9 0.7 %copy-start.5 = (f32[1024]{0:T(1024)S(1)}, f32[1024]{0:T(1024)}, u32[]{:S(2)}) copy-start(f32[1024]{0:T(1024)} %gain_ref.1) | copy-start | bytes 12292
  41.0 1.0 %copy-start.6 = (bf16[2,128,1024]{2,1,0:T(8,128)(2,1)S(1)}, bf16[2,128,1024]{2,1,0:T(8,128)(2,1)}, u32[]{:S(2)}) copy-start(bf16[2,128,1024]{2,1,0:T(8,128)(2,1)} %sq_ref.1) | copy-start | bytes 1572868
  42.0 0.7 %copy-start.7 = (s32[32,32]{1,0:T(8,128)S(1)}, s32[32,32]{1,0:T(8,128)}, u32[]{:S(2)}) copy-start(s32[32,32]{1,0:T(8,128)} %mask.1) | copy-start | bytes 12292

commit v2 on v1

--- a/solution.py
+++ b/solution.py
@@ -21,6 +21,8 @@
 NEG = -1e30
 STEP_BLOCKS = 4
 STEP = STEP_BLOCKS * TOK
+HEAD_UNROLL = 8
+U_UNROLL = 1
 SCALE = math.log2(math.e) / math.sqrt(DH)
 
 
@@ -41,9 +43,9 @@
 
 
 def linear_kernel(
-    lq_hbm, lk_hbm, lv_hbm, ld_hbm, gain_ref, sk, sv,
+    lq_hbm, lk_hbm, lv_hbm, ld_hbm, gain_hbm, sk, sv,
     lin_out, kv,
-    lq, lk, lv, ld, ks, u_send, u_recv, dec_send, dec_recv, drow_send, drow_recv,
+    lq, lk, lv, ld, gain_ref, cum_ref, colc, inv_ref, u_send, u_recv, dec_send, dec_recv, drow_send, drow_recv,
     t_send, t_recv, p_send, st, lin, sq_send, sq_recv,
     in_sem, own_sem, kv_send, kv_recv, u_ss, u_rs, d_ss, d_rs, w_ss, w_rs,
     t_ss, t_rs, p_ss, p_rs, q_ss, q_rs,
@@ -66,7 +68,7 @@
 
     loads = [
         pltpu.make_async_copy(a, b, in_sem.at[i])
-        for i, (a, b) in enumerate(((ld_hbm, ld), (lk_hbm, lk), (lv_hbm, lv), (lq_hbm, lq)))
+        for i, (a, b) in enumerate(((ld_hbm, ld), (lk_hbm, lk), (lv_hbm, lv), (lq_hbm, lq), (gain_hbm, gain_ref)))
     ]
     for c in loads:
         c.start()
@@ -84,11 +86,11 @@
     col = lax.broadcasted_iota(jnp.int32, (TOK, TOK), 1)
     tril = (row >= col).astype(F32)
     spread = (
-        lax.broadcasted_iota(jnp.int32, (HEADS, DH), 0) == lax.broadcasted_iota(jnp.int32, (HEADS, DH), 1)
+        lax.broadcasted_iota(jnp.int32, (DH, HEADS), 0) == lax.broadcasted_iota(jnp.int32, (DH, HEADS), 1)
     ).astype(F32)
-    cum = dot(tril, dot(ld[...], spread, precision=HI), precision=HI)
-    cum_t = cum.T
-    total = cum[TOK - 1 : TOK, :]
+    cum_t = dot(spread, dot_t(ld[...], tril, precision=HI), precision=HI)
+    cum_ref[...] = cum_t
+    total = cum_t.T[TOK - 1 : TOK, :]
     dec_send[...] = jnp.broadcast_to(total, (8, DH))
     dec_recv[pl.ds(z, 1)] = jnp.broadcast_to(total, (1, 8, DH))
 
@@ -154,19 +156,27 @@
     kv_own()
 
     loads[1].wait()
-    fade = jnp.exp(total - cum)
-    for h in range(HEADS):
-        hs = slice(h * DH, (h + 1) * DH)
-        ks[:, hs] = (lk[:, hs].astype(F32) * fade[:, h : h + 1]).astype(BF16)
     loads[2].wait()
-    for i in (4, 3, 5, 2, 6, 1, 7, 0):
+
+    def u_copy(i):
         h = (z + i) % NZ
-        u = dot_0(ks[:, cols(h)], lv[:, cols(h)]).astype(BF16)
-        if i:
-            u_send[pl.ds(h, 1)] = u[None]
-            start(to_seq(u_send.at[h], u_recv.at[z], u_ss.at[i], u_rs.at[z], zpeer(i)))
-        else:
-            u_recv[pl.ds(h, 1)] = u[None]
+        return to_seq(u_send.at[h], u_recv.at[z], u_ss.at[i], u_rs.at[z], y * NZ + h)
+
+    def head_update(i):
+        h = (z + i) % NZ
+        c = jnp.broadcast_to(cum_ref[pl.ds(h, 1), :], (TOK, TOK)).T
+        colc[h] = c
+        k = (lk[:, cols(h)].astype(F32) * jnp.exp(c[TOK - 1 :, :] - c)).astype(BF16)
+        return dot_0(k, lv[:, cols(h)]).astype(BF16)
+
+    def update(n, c):
+        i = n + 1
+        u_send[pl.ds((z + i) % NZ, 1)] = head_update(i)[None]
+        u_copy(i).start()
+        return c
+
+    lax.fori_loop(0, NZ - 1, update, 0, unroll=U_UNROLL)
+    u_recv[pl.ds(z, 1)] = head_update(0)[None]
 
     kv_step(1)
 
@@ -180,17 +190,21 @@
         start(to_seq(drow_send, drow_recv.at[y], w_ss.at[i], w_rs.at[y], ypeer(i)))
 
     loads[3].wait()
+    loads[4].wait()
     causal = row >= col
-    for h in range(HEADS):
-        hs = slice(h * DH, (h + 1) * DH)
-        q = lq[:, :, hs].reshape(2 * TOK, DH)
-        score = dot_t(q, lk[:, hs])
-        gap = jnp.exp(jnp.minimum(cum[:, h : h + 1] - cum_t[h : h + 1, :], 0.0))
+
+    def inside(h, c):
+        q = lq[:, :, cols(h)].reshape(2 * TOK, DH)
+        score = dot_t(q, lk[:, cols(h)])
+        gap = jnp.exp(jnp.minimum(colc[h] - cum_ref[pl.ds(h, 1), :], 0.0))
         gap = jnp.where(causal, gap, 0.0)
         w = (score.reshape(2, TOK, TOK) * gap[None]).astype(BF16).reshape(2 * TOK, TOK)
-        lin[h] = dot(w, lv[:, hs])
-        if h == 3:
-            kv_step(2)
+        lin[h] = dot(w, lv[:, cols(h)])
+        return c
+
+    lax.fori_loop(0, HEADS // 2, inside, 0, unroll=2)
+    kv_step(2)
+    lax.fori_loop(HEADS // 2, HEADS, inside, 0, unroll=2)
 
     lane = lax.broadcasted_iota(jnp.int32, (8, DH), 1)
 
@@ -236,15 +250,14 @@
         src = (z - i + NZ) % NZ
         to_seq(p_send.at[0], st.at[src], p_ss.at[i], p_rs.at[src], zpeer(i)).wait_recv()
 
-    ecum = jnp.exp(cum)
-    squares = jnp.zeros((2 * TOK, DH), F32)
-    for h in range(HEADS):
-        hs = slice(h * DH, (h + 1) * DH)
-        q = lq[:, :, hs].reshape(2 * TOK, DH)
-        f = dot(q, st[h]).reshape(2, TOK, DH) * ecum[:, h : h + 1][None]
+    def outer(h, squares):
+        q = lq[:, :, cols(h)].reshape(2 * TOK, DH)
+        f = dot(q, st[h]).reshape(2, TOK, DH) * jnp.exp(colc[h])[None]
         full = lin[h] + f.reshape(2 * TOK, DH)
         lin[h] = full
-        squares = squares + full * full
+        return squares + full * full
+
+    squares = lax.fori_loop(0, HEADS, outer, jnp.zeros((2 * TOK, DH), F32), unroll=2)
     sq = dot_t(jnp.ones((8, DH), F32), squares, precision=HI)
     sq_send[...] = sq
     sq_recv[pl.ds(hd, 1)] = sq[None]
@@ -265,10 +278,14 @@
         ).wait_recv()
     mean = jnp.sum(sq_recv[...], axis=0) * (1.0 / FEATURES)
     inv = dot_0(lax.rsqrt(mean + 1e-6), jnp.full((8, DH), 0.125, F32), precision=HI)
-    for h in range(HEADS):
-        hs = slice(h * DH, (h + 1) * DH)
-        res = lin[h] * inv * gain_ref[hs][None, :]
-        lin_out[:, :, hs] = res.astype(BF16).reshape(2, TOK, DH)
+    inv_ref[...] = inv
+
+    def scale(h, c):
+        res = lin[h] * inv_ref[...] * gain_ref[cols(h)][None, :]
+        lin_out[:, :, cols(h)] = res.astype(BF16).reshape(2, TOK, DH)
+        return c
+
+    lax.fori_loop(0, HEADS, scale, 0, unroll=2)
 
     for dz in range(NZ):
         kv_wait(block(-1, dz), 1)
@@ -279,10 +296,12 @@
         c.wait()
     for c in sends:
         c.wait_send()
+    for i in range(1, NZ):
+        u_copy(i).wait_send()
 
 
 def linear_part(lq, lk, lv, ld, gain, sk, sv):
-    hbm = pl.BlockSpec(memory_space=pl.ANY)
+    hbm = pl.BlockSpec(memory_space=pltpu.HBM)
     vmem = pl.BlockSpec(memory_space=pltpu.VMEM)
     dma = pltpu.SemaphoreType.DMA
     V = pltpu.VMEM
@@ -293,14 +312,17 @@
             jax.ShapeDtypeStruct((2, TOK, HEADS * DH), BF16),
             jax.ShapeDtypeStruct((NSEQ, 2, TOK, DH), BF16),
         ),
-        in_specs=[hbm, hbm, hbm, hbm, vmem, hbm, hbm],
-        out_specs=(vmem, hbm),
+        in_specs=[hbm, hbm, hbm, hbm, hbm, hbm, hbm],
+        out_specs=(vmem, pl.BlockSpec(memory_space=pl.ANY)),
         scratch_shapes=[
             V((2, TOK, HEADS * DH), BF16),
             V((TOK, HEADS * DH), BF16),
             V((TOK, HEADS * DH), BF16),
-            V((TOK, HEADS), F32),
-            V((TOK, HEADS * DH), BF16),
+            V((HEADS, TOK), F32),
+            V((HEADS * DH,), F32),
+            V(mat, F32),
+            V((HEADS,) + mat, F32),
+            V((2 * TOK, DH), F32),
             V((NZ,) + mat, BF16),
             V((NZ,) + mat, BF16),
             V((8, DH), F32),
@@ -314,7 +336,7 @@
             V((HEADS, 2 * TOK, DH), F32),
             V((8, 2 * TOK), F32),
             V((NX, 8, 2 * TOK), F32),
-            dma((4,)),
+            dma((5,)),
             dma((2,)),
             dma((62,)),
             dma((NSEQ, 2)),
@@ -326,7 +348,7 @@
             dma((NX,)), dma((NX,)),
         ],
         compiler_params=pltpu.CompilerParams(
-            collective_id=0, has_side_effects=True, vmem_limit_bytes=32 * 2**20
+            collective_id=0, has_side_effects=True, vmem_limit_bytes=56 * 2**20
         ),
         cost_estimate=pl.CostEstimate(flops=240_000_000, bytes_accessed=5_000_000, transcendentals=300_000),
         name="linear_and_gather",
@@ -334,128 +356,139 @@
 
 
 def softmax_kernel(
-    mask, lin_ref, sq_ref, kv,
+    mask_hbm, lin_hbm, sq_hbm, kv,
     lin_out, soft_out,
-    order, kaug, vaug, qaug, m_ref, acc, k_sem, v_sem,
+    mask, lin_ref, sq_ref, res, order, kaug, vaug, qaug, m_ref, acc, in_sem, out_sem, k_sem, v_sem,
 ):
     me = lax.axis_index("seq")
-    order[0] = me
-
-    def scan(b, n):
-        ok = jnp.logical_and(mask[me, b] == 1, b < me)
-
-        @pl.when(ok)
-        def _():
-            order[n] = b
-
-        return n + ok.astype(jnp.int32)
-
-    count = lax.fori_loop(0, NSEQ, scan, jnp.int32(1))
-    steps = (count + STEP_BLOCKS - 1) // STEP_BLOCKS
-
-    def pad(i, c):
-        order[i] = me
-        return c
-
-    lax.fori_loop(count, steps * STEP_BLOCKS, pad, 0)
 
     def rows(i, size=TOK):
         return pl.ds(pl.multiple_of(i * size, size), size)
 
-    def copies(i):
-        b = order[i]
+    def copies(i, b):
         return (
             pltpu.make_async_copy(kv.at[b, 0], kaug.at[rows(i), pl.ds(0, DH)], k_sem.at[i]),
             pltpu.make_async_copy(kv.at[b, 1], vaug.at[rows(i), pl.ds(0, DH)], v_sem.at[i]),
         )
 
-    def load(i, c):
-        for x in copies(i):
-            x.start()
-        return c
-
-    lax.fori_loop(0, steps * STEP_BLOCKS, load, 0)
+    loads = [
+        pltpu.make_async_copy(a, b, in_sem.at[i])
+        for i, (a, b) in enumerate(((mask_hbm, mask), (lin_hbm, lin_ref), (sq_hbm, sq_ref)))
+    ]
+    for c in loads:
+        c.start()
+    for c in copies(0, me):
+        c.start()
 
     row = lax.broadcasted_iota(jnp.int32, (TOK, TOK), 0)
     col = lax.broadcasted_iota(jnp.int32, (TOK, TOK), 1)
-
-    def bias(i, c):
-        kaug[rows(i), DH:] = jnp.where(i < count, 0.0, jnp.full((TOK, TOK), NEG, F32)).astype(BF16)
-        vaug[rows(i), DH:] = jnp.ones((TOK, DH), BF16)
+    pick = (row == col).astype(BF16)
+    kaug[:TOK, DH:] = jnp.where(row <= col, 0.0, NEG).astype(BF16)
+    vaug[:, DH:] = jnp.ones((NSEQ * TOK, DH), BF16)
+
+    loads[0].wait()
+    order[0] = me
+    count = jnp.int32(1)
+    for b in range(NSEQ - 1):
+        order[count] = b
+        count = count + jnp.where(b < me, mask[me, b], 0)
+    steps = (count + STEP_BLOCKS - 1) // STEP_BLOCKS
+    for n in range(STEP_BLOCKS - 1):
+        order[count + n] = me
+
+    def load(i, c):
+        for x in copies(i, order[i]):
+            x.start()
+        kaug[rows(i), DH:] = jnp.broadcast_to(jnp.where(i < count, 0.0, NEG), (TOK, TOK)).astype(BF16)
         return c
 
-    lax.fori_loop(0, steps * STEP_BLOCKS, bias, 0)
-    kaug[:TOK, DH:] = jnp.where(row <= col, 0.0, NEG).astype(BF16)
-    pick = (row == col).astype(BF16)
-    for h in range(HEADS):
-        hs = slice(h * DH, (h + 1) * DH)
+    lax.fori_loop(1, steps * STEP_BLOCKS, load, 0)
+    m_ref[...] = jnp.full_like(m_ref, -3e38)
+    acc[...] = jnp.zeros_like(acc)
+    loads[1].wait()
+    keep_lin = pltpu.make_async_copy(lin_ref, lin_out, out_sem.at[HEADS])
+    keep_lin.start()
+    loads[2].wait()
+
+    def prepare(h, c):
         for j in range(2):
-            lin = lin_ref[j, :, hs]
-            q = (sq_ref[j, :, hs].astype(F32) + lin.astype(F32)) * SCALE
+            q = (sq_ref[j, :, cols(h)].astype(F32) + lin_ref[j, :, cols(h)].astype(F32)) * SCALE
             qaug[h, j * TOK : (j + 1) * TOK, :DH] = q.astype(BF16)
             qaug[h, j * TOK : (j + 1) * TOK, DH:] = pick
-            lin_out[j, :, hs] = lin
-
-    def step(i, first):
+        return c
+
+    lax.fori_loop(0, HEADS, prepare, 0, unroll=2)
+
+    def step(i, c):
         for n in range(STEP_BLOCKS):
-            for x in copies(i * STEP_BLOCKS + n):
+            for x in copies(i * STEP_BLOCKS + n, me):
                 x.wait()
-        for h in range(HEADS):
+
+        def head(h, c):
             s = dot_t(qaug[h], kaug[rows(i, STEP), :])
-            top = jnp.max(s, axis=1, keepdims=True)
-            if not first:
-                top = jnp.maximum(m_ref[h][:, :1], top)
-                keep = jnp.exp2(m_ref[h] - top)
-            p = jnp.exp2(s - top).astype(BF16)
+            old = m_ref[h]
+            top = jnp.maximum(old, jnp.max(s, axis=1, keepdims=True))
+            m_ref[h] = top
+            keep = jnp.exp2(old - top)
+            p = jnp.concatenate(
+                [jnp.exp2(s[:, n * DH : (n + 1) * DH] - top).astype(BF16) for n in range(STEP_BLOCKS)], axis=1
+            )
             new = dot(p, vaug[rows(i, STEP), :])
-            if first:
-                acc[h] = new
-            else:
-                acc[h, :, :DH] = acc[h, :, :DH] * keep + new[:, :DH]
-                acc[h, :, DH:] = acc[h, :, DH:] * keep + new[:, DH:]
-            m_ref[h] = jnp.broadcast_to(top, (2 * TOK, DH))
-
-    step(0, True)
-
-    def rest(i, c):
-        step(i, False)
+            acc[h, :, :DH] = acc[h, :, :DH] * keep + new[:, :DH]
+            acc[h, :, DH:] = acc[h, :, DH:] * keep + new[:, DH:]
+            return c
+
+        return lax.fori_loop(0, HEADS, head, c, unroll=HEAD_UNROLL)
+
+    lax.fori_loop(0, steps, step, 0)
+
+    def out_copy(h):
+        return pltpu.make_async_copy(res.at[h], soft_out.at[:, :, cols(h)], out_sem.at[h])
+
+    def finish(h, c):
+        res[h] = (acc[h, :, :DH] / acc[h, :, DH:]).astype(BF16).reshape(2, TOK, DH)
+        out_copy(h).start()
         return c
 
-    lax.fori_loop(1, steps, rest, 0)
+    lax.fori_loop(0, HEADS, finish, 0, unroll=2)
+    keep_lin.wait()
     for h in range(HEADS):
-        hs = slice(h * DH, (h + 1) * DH)
-        out = (acc[h, :, :DH] / acc[h, :, DH:]).astype(BF16)
-        soft_out[:, :, hs] = out.reshape(2, TOK, DH)
+        out_copy(h).wait()
 
 
 def softmax_part(mask, lin, sq, kv):
     hbm = pl.BlockSpec(memory_space=pl.ANY)
-    vmem = pl.BlockSpec(memory_space=pltpu.VMEM)
     V = pltpu.VMEM
     out = jax.ShapeDtypeStruct((2, TOK, HEADS * DH), BF16)
     return pl.pallas_call(
         softmax_kernel,
         out_shape=(out, out),
-        in_specs=[pl.BlockSpec(memory_space=pltpu.SMEM), vmem, vmem, hbm],
-        out_specs=(vmem, vmem),
+        in_specs=[hbm] * 4,
+        out_specs=(hbm, hbm),
         scratch_shapes=[
-            pltpu.SMEM((NSEQ,), jnp.int32),
+            pltpu.SMEM((NSEQ, NSEQ), jnp.int32),
+            V((2, TOK, HEADS * DH), BF16),
+            V((2, TOK, HEADS * DH), BF16),
+            V((HEADS, 2, TOK, DH), BF16),
+            pltpu.SMEM((NSEQ + STEP_BLOCKS,), jnp.int32),
             V((NSEQ * TOK, 2 * DH), BF16),
             V((NSEQ * TOK, 2 * DH), BF16),
             V((HEADS, 2 * TOK, 2 * DH), BF16),
             V((HEADS, 2 * TOK, DH), F32),
             V((HEADS, 2 * TOK, 2 * DH), F32),
+            pltpu.SemaphoreType.DMA((3,)),
+            pltpu.SemaphoreType.DMA((HEADS + 1,)),
             pltpu.SemaphoreType.DMA((NSEQ,)),
             pltpu.SemaphoreType.DMA((NSEQ,)),
         ],
-        compiler_params=pltpu.CompilerParams(vmem_limit_bytes=40 * 2**20),
+        compiler_params=pltpu.CompilerParams(vmem_limit_bytes=56 * 2**20),
         cost_estimate=pl.CostEstimate(flops=6_000_000_000, bytes_accessed=5_000_000, transcendentals=6_000_000),
         name="softmax_attention",
     )(mask, lin, sq, kv)
 
 
 def local(lin_queries, lin_keys, lin_values, log_decay, norm_gain, soft_queries, soft_keys, soft_values, block_mask):
-    lin, kv = linear_part(lin_queries, lin_keys, lin_values, log_decay, norm_gain, soft_keys, soft_values)
+    lin, kv = linear_part(lin_queries, lin_keys, lin_values, log_decay.T, norm_gain, soft_keys, soft_values)
     return softmax_part(block_mask, lin, soft_queries, kv)
 
 

time: 60.3 us -> 52.4 us (0.87)
  the two profiles are of different devices: /device:TPU:249 before, /device:TPU:56 now
where the time goes in v2:
time: 52.4 us; the launch traced here: 52.2 us
  Pallas kernels  51.5 us (98%)
  between operations  0.64 us (1%)
    pallas_call x1, Pallas kernels, linear_part(): pl.pallas_call(linear_kernel, out_shape=(jax.ShapeDtypeStruct((2, TOK, HE...  39.8 us
    pallas_call x1, Pallas kernels, softmax_part(): pl.pallas_call(softmax_kernel, out_shape=(out, out), in_specs=[hbm] * 4,...  11.7 us

profile of v2, /device:TPU:56, one launch (start us, length us, event | category | flops | bytes accessed | tf_op | source)
XLA Modules:
  0.0 52.2 jit_solution(13141075271575505235)
XLA Ops:
  0.6 39.8 %linear_and_gather.1 = (bf16[2,128,1024]{2,1,0:T(8,128)(2,1)}, bf16[32,2,128,128]{3,2,1,0:T(8,128)(2,1)}) custom-call(bf16[2,128,1024]{2,1,0:T(8,128)(2,1)} %lq_hbm.1, bf16[128,1024]{1,0:T(8,128)(2,1)} %lk_hbm.1, bf16[128,1024]{1,0:T(8,128)(2,1)} %lv_hbm.1, f32[8,128]{1,0:T(8,128)} %bitcast.1, f32[1024]{0:T(1024)} %gain_hbm.1, bf16[128,128]{1,0:T(8,128)(2,1)} %sk.1, ...), custom_call_target="tpu_custom_call" | custom-call | flops 240000000 | bytes 5000000 | tf_op jit(solution)/shard_map/linear_and_gather/pallas_call | solution.py:309
  40.5 11.7 %softmax_attention.1 = (bf16[2,128,1024]{2,1,0:T(8,128)(2,1)}, bf16[2,128,1024]{2,1,0:T(8,128)(2,1)}) custom-call(s32[32,32]{1,0:T(8,128)} %mask_hbm.1, bf16[2,128,1024]{2,1,0:T(8,128)(2,1)} %get-tuple-element.4.lin_hbm, bf16[2,128,1024]{2,1,0:T(8,128)(2,1)} %sq_hbm.1, bf16[32,2,128,128]{3,2,1,0:T(8,128)(2,1)} %get-tuple-element.5.kv), custom_call_target="tpu_custom_call" | custom-call | flops 6000000000 | bytes 5000000 | tf_op jit(solution)/shard_map/softmax_attention/pallas_call | solution.py:463

commit v3 on v2

--- a/solution.py
+++ b/solution.py
@@ -19,7 +19,7 @@
 NY, NZ, NX = 4, 8, 8
 NSEQ = NY * NZ
 NEG = -1e30
-STEP_BLOCKS = 4
+STEP_BLOCKS = 8
 STEP = STEP_BLOCKS * TOK
 HEAD_UNROLL = 8
 U_UNROLL = 1
@@ -43,11 +43,11 @@
 
 
 def linear_kernel(
-    lq_hbm, lk_hbm, lv_hbm, ld_hbm, gain_hbm, sk, sv,
-    lin_out, kv,
-    lq, lk, lv, ld, gain_ref, cum_ref, colc, inv_ref, u_send, u_recv, dec_send, dec_recv, drow_send, drow_recv,
+    lq_hbm, lk_hbm, lv_hbm, ld_hbm, gain_hbm, sk, sv, sq_hbm,
+    lin_out, q_out, k_all, v_all,
+    lq, lk, lv, ld, gain_ref, sq_in, lin_res, q_res, cum_ref, colc, inv_ref, u_send, u_recv, dec_send, dec_recv, drow_send, drow_recv,
     t_send, t_recv, p_send, st, lin, sq_send, sq_recv,
-    in_sem, own_sem, kv_send, kv_recv, u_ss, u_rs, d_ss, d_rs, w_ss, w_rs,
+    in_sem, out_sem, own_sem, kv_send, kv_recv, u_ss, u_rs, d_ss, d_rs, w_ss, w_rs,
     t_ss, t_rs, p_ss, p_rs, q_ss, q_rs,
 ):
     me = lax.axis_index("seq")
@@ -68,7 +68,7 @@
 
     loads = [
         pltpu.make_async_copy(a, b, in_sem.at[i])
-        for i, (a, b) in enumerate(((ld_hbm, ld), (lk_hbm, lk), (lv_hbm, lv), (lq_hbm, lq), (gain_hbm, gain_ref)))
+        for i, (a, b) in enumerate(((ld_hbm, ld), (lk_hbm, lk), (lv_hbm, lv), (lq_hbm, lq), (gain_hbm, gain_ref), (sq_hbm, sq_in)))
     ]
     for c in loads:
         c.start()
@@ -85,14 +85,11 @@
     row = lax.broadcasted_iota(jnp.int32, (TOK, TOK), 0)
     col = lax.broadcasted_iota(jnp.int32, (TOK, TOK), 1)
     tril = (row >= col).astype(F32)
-    spread = (
-        lax.broadcasted_iota(jnp.int32, (DH, HEADS), 0) == lax.broadcasted_iota(jnp.int32, (DH, HEADS), 1)
-    ).astype(F32)
-    cum_t = dot(spread, dot_t(ld[...], tril, precision=HI), precision=HI)
+    cum_t = dot_t(ld[...], tril, precision=HI)
     cum_ref[...] = cum_t
-    total = cum_t.T[TOK - 1 : TOK, :]
-    dec_send[...] = jnp.broadcast_to(total, (8, DH))
-    dec_recv[pl.ds(z, 1)] = jnp.broadcast_to(total, (1, 8, DH))
+    total = jnp.broadcast_to(cum_t[:, TOK - 1 :], (HEADS, DH))
+    dec_send[...] = total
+    dec_recv[pl.ds(z, 1)] = total[None]
 
     pl.semaphore_wait(barrier, NZ + NY + NX - 3)
 
@@ -105,7 +102,10 @@
     for i in range(1, NZ):
         start(to_seq(dec_send, dec_recv.at[z], d_ss.at[i], d_rs.at[z], zpeer(i)))
 
-    own = [pltpu.make_async_copy(a, kv.at[me, k], own_sem.at[k]) for k, a in enumerate((sk, sv))]
+    def slot(b, k):
+        return (k_all, v_all)[k].at[pl.ds(pl.multiple_of(b * TOK, TOK), TOK)]
+
+    own = [pltpu.make_async_copy(a, slot(me, k), own_sem.at[k]) for k, a in enumerate((sk, sv))]
     for c in own:
         c.start()
     kv_count = [0]
@@ -115,10 +115,10 @@
     def kv_start(src, b, k, dev):
         n = kv_count[0]
         kv_count[0] += 1
-        start(to_seq(src, kv.at[b, k], kv_send.at[n], kv_recv.at[b, k], dev))
+        start(to_seq(src, slot(b, k), kv_send.at[n], kv_recv.at[b, k], dev))
 
     def kv_wait(b, k):
-        to_seq(kv.at[b, k], kv.at[b, k], kv_send.at[0], kv_recv.at[b, k], me).wait_recv()
+        to_seq(slot(b, k), slot(b, k), kv_send.at[0], kv_recv.at[b, k], me).wait_recv()
 
     def kv_own():
         for k, a in enumerate((sk, sv)):
@@ -133,25 +133,25 @@
                 b = zpeer(-s)
                 kv_wait(b, k)
                 if s < reach_right[k]:
-                    kv_start(kv.at[b, k], b, k, zpeer(1))
-                kv_start(kv.at[b, k], b, k, ypeer(1))
-                kv_start(kv.at[b, k], b, k, ypeer(-1))
+                    kv_start(slot(b, k), b, k, zpeer(1))
+                kv_start(slot(b, k), b, k, ypeer(1))
+                kv_start(slot(b, k), b, k, ypeer(-1))
             if s <= reach_left[k]:
                 b = zpeer(s)
                 kv_wait(b, k)
                 if s < reach_left[k]:
-                    kv_start(kv.at[b, k], b, k, zpeer(-1))
-                kv_start(kv.at[b, k], b, k, ypeer(1))
-                kv_start(kv.at[b, k], b, k, ypeer(-1))
+                    kv_start(slot(b, k), b, k, zpeer(-1))
+                kv_start(slot(b, k), b, k, ypeer(1))
+                kv_start(slot(b, k), b, k, ypeer(-1))
 
     def block(dy, dz):
         return ((y + dy + NY) % NY) * NZ + (z + dz + NZ) % NZ
 
     def kv_forward(dz):
         kv_wait(block(-1, dz), 0)
-        kv_start(kv.at[block(-1, dz), 0], block(-1, dz), 0, ypeer(1))
+        kv_start(slot(block(-1, dz), 0), block(-1, dz), 0, ypeer(1))
         kv_wait(block(1, dz), 1)
-        kv_start(kv.at[block(1, dz), 1], block(1, dz), 1, ypeer(-1))
+        kv_start(slot(block(1, dz), 1), block(1, dz), 1, ypeer(-1))
 
     kv_own()
 
@@ -191,6 +191,7 @@
 
     loads[3].wait()
     loads[4].wait()
+    loads[5].wait()
     causal = row >= col
 
     def inside(h, c):
@@ -206,12 +207,10 @@
     kv_step(2)
     lax.fori_loop(HEADS // 2, HEADS, inside, 0, unroll=2)
 
-    lane = lax.broadcasted_iota(jnp.int32, (8, DH), 1)
-
-    def of_head(v):
-        return jnp.exp(jnp.sum(jnp.where(lane == z, v, 0.0), axis=1, keepdims=True)[:1])
-
-    decay = [of_head(dec_recv[i]) for i in range(NZ)]
+    def of_head(ref, i):
+        return jnp.exp(ref[i, pl.ds(z, 1), :])
+
+    decay = [of_head(dec_recv, i) for i in range(NZ)]
     for i in range(1, NZ):
         src = (z - i + NZ) % NZ
         to_seq(u_send.at[0], u_recv.at[src], u_ss.at[i], u_rs.at[src], zpeer(i)).wait_recv()
@@ -232,7 +231,7 @@
         to_seq(t_send, t_recv.at[src], t_ss.at[i], t_rs.at[src], ypeer(i)).wait_recv()
     s = jnp.zeros((DH, DH), F32)
     for i in range(NY - 1):
-        s = jnp.where(i < y, s * of_head(drow_recv[i]) + t_recv[i].astype(F32), s)
+        s = jnp.where(i < y, s * of_head(drow_recv, i) + t_recv[i].astype(F32), s)
     for i in range(NZ):
         p_send[i] = s.astype(BF16)
         if i < NZ - 1:
@@ -243,21 +242,19 @@
     st[pl.ds(z, 1)] = p_send[pl.ds(z, 1)]
 
     kv_step(4)
-    for dz in (1, -1, 2, -2):
+    for dz in (1, -1, 2, -2, 3, -3, 4):
         kv_forward(dz)
 
-    for i in range(1, NZ):
-        src = (z - i + NZ) % NZ
-        to_seq(p_send.at[0], st.at[src], p_ss.at[i], p_rs.at[src], zpeer(i)).wait_recv()
-
-    def outer(h, squares):
+    squares = jnp.zeros((2 * TOK, DH), F32)
+    for i in (0, 4, 3, 5, 2, 6, 1, 7):
+        h = (z - i + NZ) % NZ
+        if i:
+            to_seq(p_send.at[0], st.at[h], p_ss.at[i], p_rs.at[h], zpeer(i)).wait_recv()
         q = lq[:, :, cols(h)].reshape(2 * TOK, DH)
         f = dot(q, st[h]).reshape(2, TOK, DH) * jnp.exp(colc[h])[None]
         full = lin[h] + f.reshape(2 * TOK, DH)
         lin[h] = full
-        return squares + full * full
-
-    squares = lax.fori_loop(0, HEADS, outer, jnp.zeros((2 * TOK, DH), F32), unroll=2)
+        squares = squares + full * full
     sq = dot_t(jnp.ones((8, DH), F32), squares, precision=HI)
     sq_send[...] = sq
     sq_recv[pl.ds(hd, 1)] = sq[None]
@@ -268,8 +265,6 @@
                 device_id={"head": (hd + i) % NX}, device_id_type=MESH,
             )
         )
-    for dz in (3, -3, 4):
-        kv_forward(dz)
     for i in range(1, NX):
         src = (hd - i + NX) % NX
         pltpu.make_async_remote_copy(
@@ -280,9 +275,18 @@
     inv = dot_0(lax.rsqrt(mean + 1e-6), jnp.full((8, DH), 0.125, F32), precision=HI)
     inv_ref[...] = inv
 
+    def result_copies(h):
+        return (
+            pltpu.make_async_copy(lin_res.at[h], lin_out.at[:, :, cols(h)], out_sem.at[0, h]),
+            pltpu.make_async_copy(q_res.at[h], q_out.at[:, :, cols(h)], out_sem.at[1, h]),
+        )
+
     def scale(h, c):
-        res = lin[h] * inv_ref[...] * gain_ref[cols(h)][None, :]
-        lin_out[:, :, cols(h)] = res.astype(BF16).reshape(2, TOK, DH)
+        res = (lin[h] * inv_ref[...] * gain_ref[cols(h)][None, :]).astype(BF16).reshape(2, TOK, DH)
+        lin_res[h] = res
+        q_res[h] = ((sq_in[:, :, cols(h)].astype(F32) + res.astype(F32)) * SCALE).astype(BF16)
+        for x in result_copies(h):
+            x.start()
         return c
 
     lax.fori_loop(0, HEADS, scale, 0, unroll=2)
@@ -292,6 +296,9 @@
         kv_wait(block(1, dz), 0)
         kv_wait(block(2, dz), 0)
         kv_wait(block(2, dz), 1)
+    for h in range(HEADS):
+        for x in result_copies(h):
+            x.wait()
     for c in own:
         c.wait()
     for c in sends:
@@ -300,9 +307,8 @@
         u_copy(i).wait_send()
 
 
-def linear_part(lq, lk, lv, ld, gain, sk, sv):
-    hbm = pl.BlockSpec(memory_space=pltpu.HBM)
-    vmem = pl.BlockSpec(memory_space=pltpu.VMEM)
+def linear_part(*operands):
+    hbm = pl.BlockSpec(memory_space=pl.ANY)
     dma = pltpu.SemaphoreType.DMA
     V = pltpu.VMEM
     mat = (DH, DH)
@@ -310,17 +316,22 @@
         linear_kernel,
         out_shape=(
             jax.ShapeDtypeStruct((2, TOK, HEADS * DH), BF16),
-            jax.ShapeDtypeStruct((NSEQ, 2, TOK, DH), BF16),
+            jax.ShapeDtypeStruct((2, TOK, HEADS * DH), BF16),
+            jax.ShapeDtypeStruct((NSEQ * TOK, DH), BF16),
+            jax.ShapeDtypeStruct((NSEQ * TOK, DH), BF16),
         ),
-        in_specs=[hbm, hbm, hbm, hbm, hbm, hbm, hbm],
-        out_specs=(vmem, pl.BlockSpec(memory_space=pl.ANY)),
+        in_specs=[hbm] * 8,
+        out_specs=(hbm,) * 4,
         scratch_shapes=[
             V((2, TOK, HEADS * DH), BF16),
             V((TOK, HEADS * DH), BF16),
             V((TOK, HEADS * DH), BF16),
             V((HEADS, TOK), F32),
             V((HEADS * DH,), F32),
-            V(mat, F32),
+            V((2, TOK, HEADS * DH), BF16),
+            V((HEADS, 2, TOK, DH), BF16),
+            V((HEADS, 2, TOK, DH), BF16),
+            V((HEADS, DH), F32),
             V((HEADS,) + mat, F32),
             V((2 * TOK, DH), F32),
             V((NZ,) + mat, BF16),
@@ -336,7 +347,8 @@
             V((HEADS, 2 * TOK, DH), F32),
             V((8, 2 * TOK), F32),
             V((NX, 8, 2 * TOK), F32),
-            dma((5,)),
+            dma((6,)),
+            dma((2, HEADS)),
             dma((2,)),
             dma((62,)),
             dma((NSEQ, 2)),
@@ -352,41 +364,64 @@
         ),
         cost_estimate=pl.CostEstimate(flops=240_000_000, bytes_accessed=5_000_000, transcendentals=300_000),
         name="linear_and_gather",
-    )(lq, lk, lv, ld, gain, sk, sv)
+    )(*operands)
 
 
 def softmax_kernel(
-    mask_hbm, lin_hbm, sq_hbm, kv,
+    mask_hbm, lin_hbm, q_hbm, k_all, v_all,
     lin_out, soft_out,
-    mask, lin_ref, sq_ref, res, order, kaug, vaug, qaug, m_ref, acc, in_sem, out_sem, k_sem, v_sem,
+    mask, lin_ref, res, order, kaug, vaug, qaug, m_ref, acc, in_sem, out_sem, q_sem, k_sem, v_sem,
 ):
     me = lax.axis_index("seq")
 
     def rows(i, size=TOK):
         return pl.ds(pl.multiple_of(i * size, size), size)
 
-    def copies(i, b):
+    def copies(i):
+        r = rows(i, STEP)
         return (
-            pltpu.make_async_copy(kv.at[b, 0], kaug.at[rows(i), pl.ds(0, DH)], k_sem.at[i]),
-            pltpu.make_async_copy(kv.at[b, 1], vaug.at[rows(i), pl.ds(0, DH)], v_sem.at[i]),
+            pltpu.make_async_copy(k_all.at[r], kaug.at[r, pl.ds(0, DH)], k_sem.at[i]),
+            pltpu.make_async_copy(v_all.at[r], vaug.at[r, pl.ds(0, DH)], v_sem.at[i]),
         )
 
-    loads = [
-        pltpu.make_async_copy(a, b, in_sem.at[i])
-        for i, (a, b) in enumerate(((mask_hbm, mask), (lin_hbm, lin_ref), (sq_hbm, sq_ref)))
+    fetch_mask = pltpu.make_async_copy(mask_hbm, mask, in_sem.at[0])
+    fetch_mask.start()
+    parts = me // STEP_BLOCKS + 1
+
+    def load(i, c):
+        for x in copies(i):
+            x.start()
+        return c
+
+    lax.fori_loop(0, parts, load, 0)
+    fetch_q = [
+        pltpu.make_async_copy(
+            q_hbm.at[j, :, pl.ds(h * DH, DH)], qaug.at[h, pl.ds(j * TOK, TOK), pl.ds(0, DH)], q_sem.at[h, j]
+        )
+        for h in range(HEADS)
+        for j in range(2)
     ]
-    for c in loads:
+    for c in fetch_q:
         c.start()
-    for c in copies(0, me):
-        c.start()
+    fetch_lin = pltpu.make_async_copy(lin_hbm, lin_ref, in_sem.at[1])
+    fetch_lin.start()
 
     row = lax.broadcasted_iota(jnp.int32, (TOK, TOK), 0)
     col = lax.broadcasted_iota(jnp.int32, (TOK, TOK), 1)
     pick = (row == col).astype(BF16)
-    kaug[:TOK, DH:] = jnp.where(row <= col, 0.0, NEG).astype(BF16)
-    vaug[:, DH:] = jnp.ones((NSEQ * TOK, DH), BF16)
-
-    loads[0].wait()
+    for h in range(HEADS):
+        for j in range(2):
+            qaug[h, j * TOK : (j + 1) * TOK, DH:] = pick
+    kaug[:, DH:] = jnp.zeros(((NSEQ + 1) * TOK, DH), BF16)
+    vaug[:, DH:] = jnp.ones(((NSEQ + 1) * TOK, DH), BF16)
+    kaug[NSEQ * TOK :, :DH] = jnp.zeros((TOK, DH), BF16)
+    vaug[NSEQ * TOK :, :DH] = jnp.zeros((TOK, DH), BF16)
+    kaug[NSEQ * TOK :, DH:] = jnp.full((TOK, DH), NEG, F32).astype(BF16)
+    kaug[rows(me), DH:] = jnp.where(row <= col, 0.0, NEG).astype(BF16)
+    m_ref[...] = jnp.full_like(m_ref, -3e38)
+    acc[...] = jnp.zeros_like(acc)
+
+    fetch_mask.wait()
     order[0] = me
     count = jnp.int32(1)
     for b in range(NSEQ - 1):
@@ -394,38 +429,26 @@
         count = count + jnp.where(b < me, mask[me, b], 0)
     steps = (count + STEP_BLOCKS - 1) // STEP_BLOCKS
     for n in range(STEP_BLOCKS - 1):
-        order[count + n] = me
-
-    def load(i, c):
-        for x in copies(i, order[i]):
-            x.start()
-        kaug[rows(i), DH:] = jnp.broadcast_to(jnp.where(i < count, 0.0, NEG), (TOK, TOK)).astype(BF16)
-        return c
-
-    lax.fori_loop(1, steps * STEP_BLOCKS, load, 0)
-    m_ref[...] = jnp.full_like(m_ref, -3e38)
-    acc[...] = jnp.zeros_like(acc)
-    loads[1].wait()
+        order[count + n] = NSEQ
+
+    for c in fetch_q:
+        c.wait()
+    fetch_lin.wait()
     keep_lin = pltpu.make_async_copy(lin_ref, lin_out, out_sem.at[HEADS])
     keep_lin.start()
-    loads[2].wait()
-
-    def prepare(h, c):
-        for j in range(2):
-            q = (sq_ref[j, :, cols(h)].astype(F32) + lin_ref[j, :, cols(h)].astype(F32)) * SCALE
-            qaug[h, j * TOK : (j + 1) * TOK, :DH] = q.astype(BF16)
-            qaug[h, j * TOK : (j + 1) * TOK, DH:] = pick
+
+    def arrive(i, c):
+        for x in copies(i):
+            x.wait()
         return c
 
-    lax.fori_loop(0, HEADS, prepare, 0, unroll=2)
+    lax.fori_loop(0, parts, arrive, 0)
 
     def step(i, c):
-        for n in range(STEP_BLOCKS):
-            for x in copies(i * STEP_BLOCKS + n, me):
-                x.wait()
+        places = [rows(order[i * STEP_BLOCKS + n]) for n in range(STEP_BLOCKS)]
 
         def head(h, c):
-            s = dot_t(qaug[h], kaug[rows(i, STEP), :])
+            s = dot_t(qaug[h], jnp.concatenate([kaug[r, :] for r in places], axis=0))
             old = m_ref[h]
             top = jnp.maximum(old, jnp.max(s, axis=1, keepdims=True))
             m_ref[h] = top
@@ -433,7 +456,7 @@
             p = jnp.concatenate(
                 [jnp.exp2(s[:, n * DH : (n + 1) * DH] - top).astype(BF16) for n in range(STEP_BLOCKS)], axis=1
             )
-            new = dot(p, vaug[rows(i, STEP), :])
+            new = dot(p, jnp.concatenate([vaug[r, :] for r in places], axis=0))
             acc[h, :, :DH] = acc[h, :, :DH] * keep + new[:, :DH]
             acc[h, :, DH:] = acc[h, :, DH:] * keep + new[:, DH:]
             return c
@@ -456,40 +479,42 @@
         out_copy(h).wait()
 
 
-def softmax_part(mask, lin, sq, kv):
+def softmax_part(*operands):
     hbm = pl.BlockSpec(memory_space=pl.ANY)
     V = pltpu.VMEM
     out = jax.ShapeDtypeStruct((2, TOK, HEADS * DH), BF16)
     return pl.pallas_call(
         softmax_kernel,
         out_shape=(out, out),
-        in_specs=[hbm] * 4,
+        in_specs=[hbm] * 5,
         out_specs=(hbm, hbm),
         scratch_shapes=[
             pltpu.SMEM((NSEQ, NSEQ), jnp.int32),
             V((2, TOK, HEADS * DH), BF16),
-            V((2, TOK, HEADS * DH), BF16),
             V((HEADS, 2, TOK, DH), BF16),
             pltpu.SMEM((NSEQ + STEP_BLOCKS,), jnp.int32),
-            V((NSEQ * TOK, 2 * DH), BF16),
-            V((NSEQ * TOK, 2 * DH), BF16),
+            V(((NSEQ + 1) * TOK, 2 * DH), BF16),
+            V(((NSEQ + 1) * TOK, 2 * DH), BF16),
             V((HEADS, 2 * TOK, 2 * DH), BF16),
             V((HEADS, 2 * TOK, DH), F32),
             V((HEADS, 2 * TOK, 2 * DH), F32),
-            pltpu.SemaphoreType.DMA((3,)),
+            pltpu.SemaphoreType.DMA((2,)),
             pltpu.SemaphoreType.DMA((HEADS + 1,)),
-            pltpu.SemaphoreType.DMA((NSEQ,)),
-            pltpu.SemaphoreType.DMA((NSEQ,)),
+            pltpu.SemaphoreType.DMA((HEADS, 2)),
+            pltpu.SemaphoreType.DMA((NSEQ // STEP_BLOCKS,)),
+            pltpu.SemaphoreType.DMA((NSEQ // STEP_BLOCKS,)),
         ],
         compiler_params=pltpu.CompilerParams(vmem_limit_bytes=56 * 2**20),
         cost_estimate=pl.CostEstimate(flops=6_000_000_000, bytes_accessed=5_000_000, transcendentals=6_000_000),
         name="softmax_attention",
-    )(mask, lin, sq, kv)
+    )(*operands)
 
 
 def local(lin_queries, lin_keys, lin_values, log_decay, norm_gain, soft_queries, soft_keys, soft_values, block_mask):
-    lin, kv = linear_part(lin_queries, lin_keys, lin_values, log_decay.T, norm_gain, soft_keys, soft_values)
-    return softmax_part(block_mask, lin, soft_queries, kv)
+    lin, q, k_all, v_all = linear_part(
+        lin_queries, lin_keys, lin_values, log_decay.T, norm_gain, soft_keys, soft_values, soft_queries
+    )
+    return softmax_part(block_mask, lin, q, k_all, v_all)
 
 
 def solution(mesh):

time: 52.4 us -> 49.8 us (0.950)
  Pallas kernels: 51.5 us -> 48.4 us
    pallas_call x1, Pallas kernels: 11.7 us -> 8.84 us  [softmax_part(): pl.pallas_call(softmax_kernel, out_shape=(out, out), in_specs=[hbm] * 5,...]
where the time goes in v3:
time: 49.8 us; the launch traced here: 49.1 us
  Pallas kernels  48.4 us (97%)
  between operations  0.64 us (1%)
    pallas_call x1, Pallas kernels, linear_part(): pl.pallas_call(linear_kernel, out_shape=(jax.ShapeDtypeStruct((2, TOK, HE...  39.6 us
    pallas_call x1, Pallas kernels, softmax_part(): pl.pallas_call(softmax_kernel, out_shape=(out, out), in_specs=[hbm] * 5,...  8.84 us

profile of v3, /device:TPU:56, one launch (start us, length us, event | category | flops | bytes accessed | tf_op | source)
XLA Modules:
  0.0 49.1 jit_solution(10728113772689761710)
XLA Ops:
  0.6 39.6 %linear_and_gather.1 = (bf16[2,128,1024]{2,1,0:T(8,128)(2,1)}, bf16[2,128,1024]{2,1,0:T(8,128)(2,1)}, bf16[4096,128]{1,0:T(8,128)(2,1)}, bf16[4096,128]{1,0:T(8,128)(2,1)}) custom-call(bf16[2,128,1024]{2,1,0:T(8,128)(2,1)} %lq_hbm.1, bf16[128,1024]{1,0:T(8,128)(2,1)} %lk_hbm.1, bf16[128,1024]{1,0:T(8,128)(2,1)} %lv_hbm.1, f32[8,128]{1,0:T(8,128)} %bitcast.1, ...), custom_call_target="tpu_custom_call" | custom-call | flops 240000000 | bytes 5000000 | tf_op jit(solution)/shard_map/linear_and_gather/pallas_call | solution.py:315
  40.2 8.8 %softmax_attention.1 = (bf16[2,128,1024]{2,1,0:T(8,128)(2,1)}, bf16[2,128,1024]{2,1,0:T(8,128)(2,1)}) custom-call(s32[32,32]{1,0:T(8,128)} %mask_hbm.1, bf16[2,128,1024]{2,1,0:T(8,128)(2,1)} %get-tuple-element.6.lin_hbm, bf16[2,128,1024]{2,1,0:T(8,128)(2,1)} %get-tuple-element.7.q_hbm, bf16[4096,128]{1,0:T(8,128)(2,1)} %get-tuple-element.8.k_all, ...), custom_call_target="tpu_custom_call" | custom-call | flops 6000000000 | bytes 5000000 | tf_op jit(solution)/shard_map/softmax_attention/pallas_call | solution.py:486

commit v4 on v3

--- a/solution.py
+++ b/solution.py
@@ -45,7 +45,7 @@
 def linear_kernel(
     lq_hbm, lk_hbm, lv_hbm, ld_hbm, gain_hbm, sk, sv, sq_hbm,
     lin_out, q_out, k_all, v_all,
-    lq, lk, lv, ld, gain_ref, sq_in, lin_res, q_res, cum_ref, colc, inv_ref, u_send, u_recv, dec_send, dec_recv, drow_send, drow_recv,
+    lq, lk, lv, ld, gain_ref, sq_in, lin_res, q_res, state_ref, cum_ref, colc, inv_ref, u_send, u_recv, dec_send, dec_recv, drow_send, drow_recv,
     t_send, t_recv, p_send, st, lin, sq_send, sq_recv,
     in_sem, out_sem, own_sem, kv_send, kv_recv, u_ss, u_rs, d_ss, d_rs, w_ss, w_rs,
     t_ss, t_rs, p_ss, p_rs, q_ss, q_rs,
@@ -219,8 +219,15 @@
         t = t * decay[i] + u_recv[i].astype(F32)
     t_send[...] = t.astype(BF16)
     t_recv[pl.ds(y, 1)] = t.astype(BF16)[None]
-    for i in (2, 1, 3):
-        start(to_seq(t_send, t_recv.at[y], t_ss.at[i], t_rs.at[y], ypeer(i)))
+    def total_copy(i, row_of):
+        return to_seq(t_send, t_recv.at[row_of], t_ss.at[i], t_rs.at[row_of], ypeer(i))
+
+    for i in (3, 2, 1):
+
+        @pl.when(y + i < NY)
+        def _(i=i):
+            total_copy(i, y).start()
+
 
     kv_step(3)
     kv_forward(0)
@@ -228,10 +235,19 @@
     for i in range(1, NY):
         src = (y - i + NY) % NY
         to_seq(drow_send, drow_recv.at[src], w_ss.at[i], w_rs.at[src], ypeer(i)).wait_recv()
-        to_seq(t_send, t_recv.at[src], t_ss.at[i], t_rs.at[src], ypeer(i)).wait_recv()
-    s = jnp.zeros((DH, DH), F32)
+
+        @pl.when(y >= i)
+        def _(i=i, src=src):
+            total_copy(i, src).wait_recv()
+
+    state_ref[...] = jnp.zeros((DH, DH), F32)
     for i in range(NY - 1):
-        s = jnp.where(i < y, s * of_head(drow_recv, i) + t_recv[i].astype(F32), s)
+
+        @pl.when(i < y)
+        def _(i=i):
+            state_ref[...] = state_ref[...] * of_head(drow_recv, i) + t_recv[i].astype(F32)
+
+    s = state_ref[...]
     for i in range(NZ):
         p_send[i] = s.astype(BF16)
         if i < NZ - 1:
@@ -242,7 +258,7 @@
     st[pl.ds(z, 1)] = p_send[pl.ds(z, 1)]
 
     kv_step(4)
-    for dz in (1, -1, 2, -2, 3, -3, 4):
+    for dz in (1, -1, 2, -2):
         kv_forward(dz)
 
     squares = jnp.zeros((2 * TOK, DH), F32)
@@ -255,6 +271,8 @@
         full = lin[h] + f.reshape(2 * TOK, DH)
         lin[h] = full
         squares = squares + full * full
+        if i in (3, 2, 1):
+            kv_forward({3: 3, 2: -3, 1: 4}[i])
     sq = dot_t(jnp.ones((8, DH), F32), squares, precision=HI)
     sq_send[...] = sq
     sq_recv[pl.ds(hd, 1)] = sq[None]
@@ -305,6 +323,11 @@
         c.wait_send()
     for i in range(1, NZ):
         u_copy(i).wait_send()
+    for i in range(1, NY):
+
+        @pl.when(y + i < NY)
+        def _(i=i):
+            total_copy(i, y).wait_send()
 
 
 def linear_part(*operands):
@@ -331,6 +354,7 @@
             V((2, TOK, HEADS * DH), BF16),
             V((HEADS, 2, TOK, DH), BF16),
             V((HEADS, 2, TOK, DH), BF16),
+            V(mat, F32),
             V((HEADS, DH), F32),
             V((HEADS,) + mat, F32),
             V((2 * TOK, DH), F32),

time: 49.8 us -> 51.2 us (1.028)
  the two profiles are of different devices: /device:TPU:56 before, /device:TPU:89 now
where the time goes in v4:
time: 51.2 us; the launch traced here: 50.9 us
  Pallas kernels  50.3 us (98%)
  between operations  0.64 us (1%)
    pallas_call x1, Pallas kernels, linear_part(): pl.pallas_call(linear_kernel, out_shape=(jax.ShapeDtypeStruct((2, TOK, HE...  38.5 us
    pallas_call x1, Pallas kernels, softmax_part(): pl.pallas_call(softmax_kernel, out_shape=(out, out), in_specs=[hbm] * 5,...  11.8 us

profile of v4, /device:TPU:89, one launch (start us, length us, event | category | flops | bytes accessed | tf_op | source)
XLA Modules:
  0.0 50.9 jit_solution(210933348085032572)
XLA Ops:
  0.6 38.5 %linear_and_gather.1 = (bf16[2,128,1024]{2,1,0:T(8,128)(2,1)}, bf16[2,128,1024]{2,1,0:T(8,128)(2,1)}, bf16[4096,128]{1,0:T(8,128)(2,1)}, bf16[4096,128]{1,0:T(8,128)(2,1)}) custom-call(bf16[2,128,1024]{2,1,0:T(8,128)(2,1)} %lq_hbm.1, bf16[128,1024]{1,0:T(8,128)(2,1)} %lk_hbm.1, bf16[128,1024]{1,0:T(8,128)(2,1)} %lv_hbm.1, f32[8,128]{1,0:T(8,128)} %bitcast.1, ...), custom_call_target="tpu_custom_call" | custom-call | flops 240000000 | bytes 5000000 | tf_op jit(solution)/shard_map/linear_and_gather/pallas_call | solution.py:338
  39.2 11.8 %softmax_attention.1 = (bf16[2,128,1024]{2,1,0:T(8,128)(2,1)}, bf16[2,128,1024]{2,1,0:T(8,128)(2,1)}) custom-call(s32[32,32]{1,0:T(8,128)} %mask_hbm.1, bf16[2,128,1024]{2,1,0:T(8,128)(2,1)} %get-tuple-element.6.lin_hbm, bf16[2,128,1024]{2,1,0:T(8,128)(2,1)} %get-tuple-element.7.q_hbm, bf16[4096,128]{1,0:T(8,128)(2,1)} %get-tuple-element.8.k_all, ...), custom_call_target="tpu_custom_call" | custom-call | flops 6000000000 | bytes 5000000 | tf_op jit(solution)/shard_map/softmax_attention/pallas_call | solution.py:510
